TPU v7x, 256 devices: a whole 4x4x8 slice. The times are simulated.
256 devices in a mesh: dp: 4 (over z_lo), text: 8 (over y, core), image: 8 (over x, z_hi).
Axes of the slice: x: 4, y: 4, z: 8 (z_hi: 2, z_lo: 4; z = z_hi * 4 + z_lo), core: 2. Of those that a mesh axis runs over, the one named last changes fastest.
Arguments:
- tokens: bfloat16 [32768, 4096], P(('dp', 'text', 'image')), may hold values from -24 to 24
- modality: int32 [32768], P(('dp', 'text', 'image')), may hold values from 0 to 1, as said below
- gain_text: float32 [4096], replicated, may hold values from 0.1 to 1.9
- gain_image: float32 [4096], replicated, may hold values from 0.1 to 1.9
- text_weight: bfloat16 [4096, 4096], P(('dp', 'image'), 'text'), may hold values from -0.0234375 to 0.0234375
- image_weight: bfloat16 [4096, 4096], P(('dp', 'text'), 'image'), may hold values from -0.0234375 to 0.0234375
- cotangent: bfloat16 [32768, 4096], P(('dp', 'text', 'image')), may hold values from -3 to 3
Outputs:
- queries: bfloat16 [32768, 4096], P(('dp', 'text', 'image'))
- token_grads: bfloat16 [32768, 4096], P(('dp', 'text', 'image'))
- text_weight_grad: float32 [4096, 4096], P(('dp', 'image'), 'text')
- image_weight_grad: float32 [4096, 4096], P(('dp', 'text'), 'image')
- text_gain_grad: float32 [4096], replicated
- image_gain_grad: float32 [4096], replicated
Inputs may be any that keep to these rules, and one draw needn't show every extreme that they name: `modality`: entry 0 marks a text token and 1 an image token. In each aligned block of 128 positions at most 72 entries are 0 and at most 72 are 1; both bounds are met with equality in some blocks of every draw.
All inputs are finite; a program needn't handle non-finite values.
Results may differ from a plain program's by a relative error of at most 0.018.
Values may be sent and summed in bfloat16 or wider, within the bound.
A program may use at most 128 MiB of HBM per device.

v0:
```python
import jax
import jax.numpy as jnp
from jax import lax
from jax.sharding import PartitionSpec as P

CAP = 72


EPSILON = 1e-05


def add_rows(left_rows, weight_rows):
    return jnp.dot(left_rows, weight_rows, preferred_element_type=jnp.float32)


def back_rows(upstream, weight_rows):
    return lax.dot_general(
        upstream, weight_rows, (((1,), (1,)), ((), ())), preferred_element_type=jnp.float32
    )


def weight_term(left_rows, upstream):
    return lax.dot_general(
        left_rows, upstream, (((0,), (0,)), ((), ())), preferred_element_type=jnp.float32
    )


def rounded(values):
    return lax.optimization_barrier(values.astype(jnp.bfloat16)).astype(jnp.float32)


def shards(tokens, modality, gain_text, gain_image, text_weight, image_weight, cotangent):
    held_rows = tokens.shape[0]
    as_float = tokens.astype(jnp.float32)
    inv_rms = lax.rsqrt(jnp.mean(as_float * as_float, axis=1) + EPSILON)
    unit_rows = as_float * inv_rms[:, None]
    is_text = modality == 0
    row_gains = jnp.where(is_text[:, None], gain_text[None, :], gain_image[None, :])
    normed = (unit_rows * row_gains).astype(jnp.bfloat16)
    text_flags = is_text.astype(jnp.int32)
    text_count = jnp.sum(text_flags)
    image_count = held_rows - text_count
    slot_ids = jnp.arange(CAP, dtype=jnp.int32)
    text_order = jnp.argsort(modality, stable=True)[:CAP]
    image_order = jnp.argsort(1 - modality, stable=True)[:CAP]
    text_live = (slot_ids < text_count)[:, None]
    image_live = (slot_ids < image_count)[:, None]
    text_slot = jnp.clip(jnp.cumsum(text_flags) - 1, 0, CAP - 1)
    image_slot = jnp.clip(jnp.cumsum(1 - text_flags) - 1, 0, CAP - 1)
    text_block = jnp.where(text_live, normed[text_order], jnp.zeros((), jnp.bfloat16))
    image_block = jnp.where(image_live, normed[image_order], jnp.zeros((), jnp.bfloat16))
    text_rows = lax.all_gather(text_block, "text", axis=0, tiled=True)
    image_rows = lax.all_gather(image_block, "image", axis=0, tiled=True)
    text_cols = add_rows(
        text_rows, lax.all_gather(text_weight, ("dp", "image"), axis=0, tiled=True)
    )
    image_cols = add_rows(
        image_rows, lax.all_gather(image_weight, ("dp", "text"), axis=0, tiled=True)
    )
    text_out = lax.all_to_all(
        text_cols.astype(jnp.bfloat16), "text", split_axis=0, concat_axis=1, tiled=True
    )
    image_out = lax.all_to_all(
        image_cols.astype(jnp.bfloat16), "image", split_axis=0, concat_axis=1, tiled=True
    )
    queries = jnp.where(is_text[:, None], text_out[text_slot], image_out[image_slot])
    text_up = jnp.where(text_live, cotangent[text_order], jnp.zeros((), jnp.bfloat16))
    image_up = jnp.where(image_live, cotangent[image_order], jnp.zeros((), jnp.bfloat16))
    text_grad_cols = lax.all_to_all(text_up, "text", split_axis=1, concat_axis=0, tiled=True)
    image_grad_cols = lax.all_to_all(image_up, "image", split_axis=1, concat_axis=0, tiled=True)
    text_weight_grad = lax.psum_scatter(
        weight_term(text_rows, text_grad_cols), ("dp", "image"), scatter_dimension=0, tiled=True
    )
    image_weight_grad = lax.psum_scatter(
        weight_term(image_rows, image_grad_cols), ("dp", "text"), scatter_dimension=0, tiled=True
    )
    text_part = back_rows(
        text_grad_cols, lax.all_gather(text_weight, ("dp", "image"), axis=0, tiled=True)
    )
    image_part = back_rows(
        image_grad_cols, lax.all_gather(image_weight, ("dp", "text"), axis=0, tiled=True)
    )
    text_back = lax.psum_scatter(
        rounded(text_part).astype(jnp.bfloat16), "text", scatter_dimension=0, tiled=True
    ).astype(jnp.float32)
    image_back = lax.psum_scatter(
        rounded(image_part).astype(jnp.bfloat16), "image", scatter_dimension=0, tiled=True
    ).astype(jnp.float32)
    normed_grad = jnp.where(is_text[:, None], text_back[text_slot], image_back[image_slot])
    scaled_grad = normed_grad * row_gains
    along_unit = jnp.mean(scaled_grad * unit_rows, axis=1)
    token_grads = (inv_rms[:, None] * (scaled_grad - unit_rows * along_unit[:, None])).astype(
        jnp.bfloat16
    )
    gain_term = normed_grad * unit_rows
    text_term = jnp.sum(jnp.where(is_text[:, None], gain_term, 0.0), axis=0)
    image_term = jnp.sum(jnp.where(is_text[:, None], 0.0, gain_term), axis=0)
    gain_grads = lax.psum((text_term, image_term), ("dp", "text", "image"))
    return (queries, token_grads, text_weight_grad, image_weight_grad, gain_grads[0], gain_grads[1])


def solution(mesh):
    placed = (
        P(("dp", "text", "image"), None),
        P(("dp", "text", "image")),
        P(),
        P(),
        P(("dp", "image"), "text"),
        P(("dp", "text"), "image"),
        P(("dp", "text", "image"), None),
    )
    return jax.shard_map(
        shards,
        mesh=mesh,
        in_specs=placed,
        out_specs=(
            P(("dp", "text", "image"), None),
            P(("dp", "text", "image"), None),
            P(("dp", "image"), "text"),
            P(("dp", "text"), "image"),
            P(),
            P(),
        ),
        check_vma=False,
    )
```

profile of v0, /device:TPU:2, one launch (start us, length us, event | category | flops | bytes accessed | tf_op | source)
XLA Modules:
  0.0 1348.1 jit_solution(4085219509390587710)
XLA Ops:
  8.7 1.3 subtract_bitcast_fusion
  10.7 2.5 sort.32
  14.3 36.7 %all_to_all.70 = bf16[72,8,512]{2,0,1:T(8,128)(2,1)S(1)} all-to-all(bf16[72,8,512]{2,0,1:T(8,128)(2,1)S(1)} %bitcast_select_fusion), channel_id=1, replica_groups=mesh['dp'=4,'text'=8,'image'=8] {'image'}, dimensions={1} | all-to-all | bytes 1179648 | tf_op jit(solution)/shard_map/all_to_all | solution.py:70
  51.0 33.6 %all-gather.11.cloned.1.call-done = bf16[4096,512]{1,0:T(8,128)(2,1)} async-done(((bf16[128,512]{1,0:T(8,128)(2,1)}), bf16[4096,512]{1,0:T(8,128)(2,1)}) %all-gather.11.cloned.1.call-update) | async-done | bytes 4194320 | tf_op jit(solution)/shard_map/all_gather | solution.py:58
  84.5 6.5 convolution_convert_fusion
  91.7 2.5 sort.31
  95.9 14.4 %all_to_all.71 = bf16[72,8,512]{2,0,1:T(8,128)(2,1)S(1)} all-to-all(bf16[72,8,512]{2,0,1:T(8,128)(2,1)S(1)} %bitcast_select_fusion.1), channel_id=1, replica_groups=mesh['dp'=4,'text'=8,'image'=8] {'text'}, dimensions={1} | all-to-all | bytes 1179648 | tf_op jit(solution)/shard_map/all_to_all | solution.py:69
  110.4 228.4 %all-gather.7.cloned.1.call-done = bf16[4096,512]{1,0:T(8,128)(2,1)} async-done(((bf16[128,512]{1,0:T(8,128)(2,1)}), bf16[4096,512]{1,0:T(8,128)(2,1)}) %all-gather.7.cloned.1.call-update) | async-done | bytes 4194320 | tf_op jit(solution)/shard_map/all_gather | solution.py:55
  338.7 6.4 convolution_convert_fusion.1
  346.7 137.3 %reduce-scatter.7.cloned.1.call-done = bf16[72,4096]{1,0:T(8,128)(2,1)} async-done(((bf16[576,4096]{1,0:T(8,128)(2,1)}), bf16[72,4096]{1,0:T(8,128)(2,1)}) %reduce-scatter.7.cloned.1.call-update) | async-done | bytes 589840 | tf_op jit(solution)/shard_map/reduce_scatter | solution.py:86
  484.0 1.2 convert_element_type.42
  485.2 2.6 gather_fusion.7
  487.7 36.7 %reduce-scatter.5.cloned.1.call-done = bf16[72,4096]{1,0:T(8,128)(2,1)} async-done(((bf16[576,4096]{1,0:T(8,128)(2,1)}), bf16[72,4096]{1,0:T(8,128)(2,1)}) %reduce-scatter.5.cloned.1.call-update) | async-done | bytes 589840 | tf_op jit(solution)/shard_map/reduce_scatter | solution.py:83
  524.4 1.2 convert_element_type.40
  525.6 2.6 gather_fusion.5
  528.2 3.4 select_reduce_fusion
  531.6 1.8 fusion.6
  537.2 34.1 %all-gather.5.cloned.1.call-done = bf16[576,4096]{1,0:T(8,128)(2,1)} async-done(((bf16[72,4096]{1,0:T(8,128)(2,1)}), bf16[576,4096]{1,0:T(8,128)(2,1)}) %all-gather.5.cloned.1.call-update) | async-done | bytes 4718608 | tf_op jit(solution)/shard_map/all_gather | solution.py:52
  571.3 8.1 fusion.11
  579.7 108.2 %all-gather.9.cloned.1.call-done = bf16[576,4096]{1,0:T(8,128)(2,1)} async-done(((bf16[72,4096]{1,0:T(8,128)(2,1)}), bf16[576,4096]{1,0:T(8,128)(2,1)}) %all-gather.9.cloned.1.call-update) | async-done | bytes 4718608 | tf_op jit(solution)/shard_map/all_gather | solution.py:53
  687.9 8.1 fusion.12
  696.0 7.2 convolution_convert_fusion.3
  703.3 4.3 all-to-all-start
  707.6 7.1 convolution_convert_fusion.2
  714.6 4.0 all-to-all-done
  718.6 5.2 all-to-all-start.1
  723.8 149.7 %all-reduce = (f32[4096]{0:T(1024)}, f32[4096]{0:T(1024)}) all-reduce(f32[4096]{0:T(1024)S(1)} %get-tuple-element.11, f32[4096]{0:T(1024)S(1)} %get-tuple-element.10), channel_id=1, replica_groups=mesh['dp'=4,'text'=8,'image'=8] {'dp','text','image'}, use_global_device_ids=true, to_apply=%region_12.13 | all-reduce | flops 8192 | bytes 65536 | tf_op jit(solution)/shard_map/psum | solution.py:98
  873.5 1.2 gather_fusion.1
  874.8 2.2 gather_fusion.3
  877.0 2.4 broadcast_select_fusion.1
  879.3 300.9 %reduce-scatter.9.cloned.1.call-done = f32[128,512]{1,0:T(8,128)} async-done(((f32[4096,512]{1,0:T(8,128)}), f32[128,512]{1,0:T(8,128)}) %reduce-scatter.9.cloned.1.call-update) | async-done | bytes 262160 | tf_op jit(solution)/shard_map/reduce_scatter | solution.py:71
  1180.2 161.1 %reduce-scatter.11.cloned.1.call-done = f32[128,512]{1,0:T(8,128)} async-done(((f32[4096,512]{1,0:T(8,128)}), f32[128,512]{1,0:T(8,128)}) %reduce-scatter.11.cloned.1.call-update) | async-done | bytes 262160 | tf_op jit(solution)/shard_map/reduce_scatter | solution.py:74
  (59 shorter events, 10.5 us)
Async XLA Ops:
  7.2 6.1 copy-start
  7.2 77.3 %all-gather.11.cloned.1.call-start = ((), (), s32[]{:S(2)}) async-start(), calls=%async_computation.11 | async-start | bytes 4325376 | tf_op jit(solution)/shard_map/all_gather | solution.py:58
  7.9 330.8 %all-gather.7.cloned.1.call-start = ((), (), s32[]{:S(2)}) async-start(), calls=%async_computation.9 | async-start | bytes 4325376 | tf_op jit(solution)/shard_map/all_gather | solution.py:55
  8.7 475.3 %reduce-scatter.7.cloned.1.call-start = ((), (), s32[]{:S(2)}) async-start(), calls=%async_computation.13 | async-start | bytes 5308416 | tf_op jit(solution)/shard_map/reduce_scatter | solution.py:86
  91.0 0.7 copy-start.5
  91.1 433.4 %reduce-scatter.5.cloned.1.call-start = ((), (), s32[]{:S(2)}) async-start(), calls=%async_computation.12 | async-start | bytes 5308416 | tf_op jit(solution)/shard_map/reduce_scatter | solution.py:83
  345.2 1.2 copy-start.2
  345.2 226.2 %all-gather.5.cloned.1.call-start = ((), (), s32[]{:S(2)}) async-start(), calls=%async_computation.8 | async-start | bytes 5308416 | tf_op jit(solution)/shard_map/all_gather | solution.py:52
  525.6 2.6 copy-start.3
  525.6 2.6 copy-start.4
  535.2 152.7 %all-gather.9.cloned.1.call-start = ((), (), s32[]{:S(2)}) async-start(), calls=%async_computation.10 | async-start | bytes 5308416 | tf_op jit(solution)/shard_map/all_gather | solution.py:53
  537.2 643.0 %reduce-scatter.9.cloned.1.call-start = ((), (), s32[]{:S(2)}) async-start(), calls=%async_computation.14 | async-start | bytes 8650752 | tf_op jit(solution)/shard_map/reduce_scatter | solution.py:71
  579.5 761.8 %reduce-scatter.11.cloned.1.call-start = ((), (), s32[]{:S(2)}) async-start(), calls=%async_computation.15 | async-start | bytes 8650752 | tf_op jit(solution)/shard_map/reduce_scatter | solution.py:74
  703.3 15.3 %all-to-all-start = ((bf16[8,72,512]{2,1,0:T(8,128)(2,1)}), bf16[8,72,512]{2,1,0:T(8,128)(2,1)S(1)}, u32[]{:S(2)}, u32[]{:S(2)}) async-start(bf16[8,72,512]{2,1,0:T(8,128)(2,1)} %bitcast), calls=%async_computation | async-start | bytes 1179648 | tf_op jit(solution)/shard_map/all_to_all | solution.py:60
  718.6 156.1 %all-to-all-start.1 = ((bf16[8,72,512]{2,1,0:T(8,128)(2,1)}), bf16[8,72,512]{2,1,0:T(8,128)(2,1)S(1)}, u32[]{:S(2)}, u32[]{:S(2)}) async-start(bf16[8,72,512]{2,1,0:T(8,128)(2,1)} %bitcast.3), calls=%async_computation.1 | async-start | bytes 1179648 | tf_op jit(solution)/shard_map/all_to_all | solution.py:63
  874.8 466.5 %copy-start.1 = (bf16[128,4096]{1,0:T(8,128)(2,1)S(1)}, bf16[128,4096]{1,0:T(8,128)(2,1)}, u32[]{:S(2)}) copy-start(bf16[128,4096]{1,0:T(8,128)(2,1)} %param.13) | copy-start | bytes 3145732
Sparse Core Ops, SparseCore 0:
  9.9 74.6 all-gather.10
  86.3 252.3 all-gather.6
  343.0 140.9 reduce-scatter.6
  486.6 37.8 reduce-scatter.4
  535.3 35.9 all-gather.4
  574.1 113.7 all-gather.8
  691.2 488.9 reduce-scatter.8
  1183.5 157.7 reduce-scatter.10
where the time goes:
time: 1350 us
  waiting for transfers between devices  1050 us (78%)
  blocking collectives  201 us (15%)
  matrix products  43.5 us (3%)
  other arithmetic  19.9 us (1%)
  between operations  15 us (1%)
    reduce_scatter x1, waiting for transfers between devices, shards(): lax.psum_scatter(weight_term(text_rows, text_grad_cols), ('dp', 'image'),...  301 us
    all_gather x1, waiting for transfers between devices, shards(): lax.all_gather(text_weight, ('dp', 'image'), axis=0, tiled=True)  228 us
    reduce_scatter x1, waiting for transfers between devices, shards(): lax.psum_scatter(weight_term(image_rows, image_grad_cols), ('dp', 'text')...  161 us
    psum x1, blocking collectives, shards(): gain_grads = lax.psum((text_term, image_term), ('dp', 'text', 'image'))  150 us
    reduce_scatter x1, waiting for transfers between devices, shards(): lax.psum_scatter(rounded(image_part).astype(jnp.bfloat16), 'image', scatt...  137 us
    all_gather x1, waiting for transfers between devices, shards(): image_rows = lax.all_gather(image_block, 'image', axis=0, tiled=True)  108 us
    reduce_scatter x1, waiting for transfers between devices, shards(): lax.psum_scatter(rounded(text_part).astype(jnp.bfloat16), 'text', scatter...  36.7 us
    all_to_all x1, blocking collectives, shards(): lax.all_to_all(image_up, 'image', split_axis=1, concat_axis=0, tiled=True)  36.7 us
  transfers between devices with their start and end apart: 10, of which 9 were waited for; matrix products, arithmetic and copies ran while one was open for 5% of the time, Pallas kernels for 0%

commit v1 on v0

v1 whole, which is shorter than its diff:
```python
import functools

import jax
import jax.numpy as jnp
from jax import lax
from jax.experimental import pallas as pl
from jax.experimental.pallas import tpu as pltpu
from jax.sharding import PartitionSpec as P

MESH = pl.DeviceIdType.MESH
CAP = 72
EPSILON = 1e-05
F32 = jnp.float32
BF16 = jnp.bfloat16


def dot_nn(left, right):
    return jnp.dot(left, right, preferred_element_type=F32)


def dot_nt(left, right):
    return lax.dot_general(left, right, (((1,), (1,)), ((), ())), preferred_element_type=F32)


def dot_tn(left, right):
    return lax.dot_general(left, right, (((0,), (0,)), ((), ())), preferred_element_type=F32)


def layer(
    dims,
    mod_ref, gt_ref, gi_ref, tok_ref, cot_ref, wt_ref, wi_ref,
    q_out, tg_out, dwt_out, dwi_out, ggt_out, ggi_out,
    pick, place, flag, inv, work, gacc,
    xs, gs, xall, gall, w, qp, dp, qr, dr, qf, df,
    dw_own, dw_peer, dw_sum, dw_z,
    g_core, g_b, g_z, g_c,
    send, x1, x2, g1, g2, w1, w2, q1, q2, d1, d2, e1, e2, s1, s2, s3, s4,
):
    S, ZL, T, R, DS, ES = dims
    NZ = 2 * ZL
    CH = DS // ZL
    WR, WC = CH // 2, ES // 2
    D, E = DS * S, ES * S
    GR = DS // 128
    zl, text, image = lax.axis_index("dp"), lax.axis_index("text"), lax.axis_index("image")
    y, core = lax.div(text, 2), lax.rem(text, 2)
    x, zh = lax.div(image, 2), lax.rem(image, 2)
    z = zh * ZL + zl

    def cc(m):
        return x + (y - x) * m

    def bc(m):
        return y + (x - y) * m

    def along_c(m, k):
        return (zl, lax.rem(text + 2 * k * m, 2 * S), lax.rem(image + 2 * k * (1 - m), 2 * S))

    def along_b(m, k):
        return (zl, lax.rem(text + 2 * k * (1 - m), 2 * S), lax.rem(image + 2 * k * m, 2 * S))

    def along_z(k):
        to = lax.rem(z + k, NZ)
        return (lax.rem(to, ZL), text, 2 * x + lax.div(to, ZL))

    partner = (zl, text + 1 - 2 * core, image)

    def push(src, dst, send_sem, recv_sem, device):
        return pltpu.make_async_remote_copy(
            src_ref=src, dst_ref=dst, send_sem=send_sem, recv_sem=recv_sem,
            device_id=device, device_id_type=MESH,
        )

    def arrived(dst, recv_sem):
        push(dst, dst, send.at[0], recv_sem, partner).wait_recv()

    def sent(src, send_sem):
        push(src, src, send_sem, x1.at[0], partner).wait_send()

    barrier = pltpu.get_barrier_semaphore()

    @pl.loop(1, S)
    def _(k):
        pl.semaphore_signal(barrier, inc=1, device_id=along_c(0, k), device_id_type=MESH)
        pl.semaphore_signal(barrier, inc=1, device_id=along_b(0, k), device_id_type=MESH)

    @pl.loop(1, NZ)
    def _(k):
        pl.semaphore_signal(barrier, inc=1, device_id=along_z(k), device_id_type=MESH)

    pl.semaphore_signal(barrier, inc=1, device_id=partner, device_id_type=MESH)

    rows = lax.broadcasted_iota(jnp.int32, (T, T), 0)
    cols = lax.broadcasted_iota(jnp.int32, (T, T), 1)
    flag_row = jnp.where(mod_ref[...] == 0, 1.0, 0.0)
    wide = jnp.broadcast_to(flag_row, (T, T))
    flag_col = jnp.sum(jnp.where(rows == cols, wide, 0.0), axis=1, keepdims=True)
    rank_col = jnp.sum(jnp.where(cols < rows, wide, 0.0), axis=1, keepdims=True)
    tall = jnp.broadcast_to(flag_col, (T, T))
    rank_row = jnp.sum(jnp.where(rows < cols, tall, 0.0), axis=0, keepdims=True)
    flag[...] = flag_col
    slot = lax.broadcasted_iota(jnp.int32, (R, T), 0).astype(F32)
    spot = lax.broadcasted_iota(jnp.int32, (R, T), 1).astype(F32)
    pick[0] = jnp.where((rank_row == slot) & (flag_row > 0.5), 1.0, 0.0).astype(BF16)
    pick[1] = jnp.where((spot - rank_row == slot) & (flag_row < 0.5), 1.0, 0.0).astype(BF16)
    slot = lax.broadcasted_iota(jnp.int32, (T, R), 1).astype(F32)
    spot = lax.broadcasted_iota(jnp.int32, (T, R), 0).astype(F32)
    place[0] = jnp.where((rank_col == slot) & (flag_col > 0.5), 1.0, 0.0).astype(BF16)
    place[1] = jnp.where((spot - rank_col == slot) & (flag_col < 0.5), 1.0, 0.0).astype(BF16)

    def w_at(m, from_z, from_core):
        from_zh, from_zl = lax.div(from_z, ZL), lax.rem(from_z, ZL)
        half = from_core + (from_zh - from_core) * m
        row = 2 * from_zl + from_zh + (from_core - from_zh) * m
        return w.at[m * 2 + half, pl.ds(pl.multiple_of(row * WR, WR), WR), :]

    w_at(0, z, core)[...] = wt_ref[...]
    w_at(1, z, core)[...] = wi_ref[...]

    pl.semaphore_wait(barrier, 2 * (S - 1) + NZ)

    @pl.loop(0, 2)
    def _(m):
        mine = w_at(m, z, core)
        push(mine, mine, send.at[17 + m], w2.at[m * NZ], partner).start()

        @pl.loop(1, NZ)
        def _(k):
            push(mine, mine, send.at[17 + m], w1.at[m * NZ + k], along_z(k)).start()

    @pl.loop(0, 2 * S)
    def _(i):
        m, b = lax.div(i, S), lax.rem(i, S)
        part = cot_ref[:, pl.ds(pl.multiple_of(b * ES, ES), ES)]
        gs[i] = dot_nn(pick[m], part).astype(BF16)

    @pl.loop(0, 2)
    def _(m):
        mine = (m * S + bc(m)) * S + cc(m)
        gall[mine] = gs[m * S + bc(m)]

        @pl.loop(1, S)
        def _(j):
            to = lax.rem(bc(m) + j, S)
            push(gs.at[m * S + to], gall.at[mine], send.at[2], g1.at[m * S + j], along_b(m, j)).start()

        @pl.loop(1, S)
        def _(k):
            push(
                gall.at[mine], gall.at[mine], send.at[3], g2.at[m * S * S + k], along_c(m, k)
            ).start()

    squares = jnp.zeros((T, CH), F32)
    for i in range(S * ZL):
        part = tok_ref[:, i * CH:(i + 1) * CH].astype(F32)
        squares = squares + part * part
    inv_rms = lax.rsqrt(jnp.sum(squares, axis=1, keepdims=True) / D + EPSILON)
    inv[...] = inv_rms

    @pl.loop(0, S * ZL)
    def _(i):
        c, zq = lax.div(i, ZL), lax.rem(i, ZL)
        at = pl.ds(pl.multiple_of(zq * (S * CH) + c * CH, CH), CH)
        to = pl.ds(pl.multiple_of(zq * CH, CH), CH)
        unit = tok_ref[:, at].astype(F32) * inv[...]
        gains = jnp.where(flag[...] > 0.5, gt_ref[:, at], gi_ref[:, at])
        normed = (unit * gains).astype(BF16)
        xs[c, :, to] = dot_nn(pick[0], normed).astype(BF16)
        xs[S + c, :, to] = dot_nn(pick[1], normed).astype(BF16)

    @pl.loop(0, 2)
    def _(m):
        mine = (m * S + bc(m)) * S + cc(m)
        xall[mine] = xs[m * S + cc(m)]

        @pl.loop(1, S)
        def _(k):
            to = lax.rem(cc(m) + k, S)
            push(xs.at[m * S + to], xall.at[mine], send.at[4], x1.at[m * S + k], along_c(m, k)).start()

        @pl.loop(1, S)
        def _(j):
            push(
                xall.at[mine], xall.at[mine], send.at[5], x2.at[m * S * S + j * S], along_b(m, j)
            ).start()

    @pl.loop(1, S)
    def _(j):
        @pl.loop(0, 2)
        def _(m):
            block = gall.at[(m * S + lax.rem(bc(m) + S - j, S)) * S + cc(m)]
            arrived(block, g1.at[m * S + j])

            @pl.loop(1, S)
            def _(k):
                push(block, block, send.at[3], g2.at[(m * S + j) * S + k], along_c(m, k)).start()

    @pl.loop(1, S)
    def _(k):
        @pl.loop(0, 2)
        def _(m):
            block = xall.at[(m * S + bc(m)) * S + lax.rem(cc(m) + S - k, S)]
            arrived(block, x1.at[m * S + k])

            @pl.loop(1, S)
            def _(j):
                push(block, block, send.at[5], x2.at[(m * S + j) * S + k], along_b(m, j)).start()

    @pl.loop(1, NZ)
    def _(k):
        @pl.loop(0, 2)
        def _(m):
            block = w_at(m, lax.rem(z + NZ - k, NZ), core)
            arrived(block, w1.at[m * NZ + k])
            push(block, block, send.at[19 + m], w2.at[m * NZ + k], partner).start()

    @pl.loop(0, NZ)
    def _(k):
        @pl.loop(0, 2)
        def _(m):
            arrived(w_at(m, lax.rem(z + NZ - k, NZ), 1 - core), w2.at[m * NZ + k])

    @pl.loop(0, 2)
    def _(m):
        @pl.loop(0, S)
        def _(j):
            b = lax.rem(bc(m) + S - j, S)
            base = (m * S + b) * S

            @pl.when(j > 0)
            def _():
                @pl.loop(0, S)
                def _(k):
                    c = lax.rem(cc(m) + S - k, S)
                    arrived(xall.at[base + c], x2.at[(m * S + j) * S + k])

            block = xall[pl.ds(base, S)].reshape(S * R, DS)
            for half in range(2):
                part = dot_nn(block, w[m * 2 + half]).astype(BF16)
                qp[pl.ds(base, S), :, half * WC:(half + 1) * WC] = part.reshape(S, R, WC)

            @pl.loop(1, S)
            def _(k):
                c = lax.rem(cc(m) + k, S)
                at = (m * (S - 1) + k - 1) * S + b
                push(
                    qp.at[base + c], qr.at[at], send.at[7], q1.at[(m * S + k) * S + b], along_c(m, k)
                ).start()

    gacc[...] = jnp.zeros_like(gacc)

    @pl.loop(0, 2)
    def _(m):
        @pl.loop(1, S)
        def _(k):
            c = lax.rem(cc(m) + S - k, S)

            @pl.loop(0, S)
            def _(j):
                b = lax.rem(bc(m) + S - j, S)
                arrived(gall.at[(m * S + b) * S + c], g2.at[(m * S + j) * S + k])

        @pl.loop(1, S + 1)
        def _(j):
            b = lax.rem(bc(m) + j, S)
            base = (m * S + b) * S
            for part in range(2):
                at = slice(part * (DS // 2), (part + 1) * (DS // 2))
                total = dot_nt(
                    gall[pl.ds(base, S), :, :WC].reshape(S * R, WC), w[m * 2, at, :]
                ) + dot_nt(
                    gall[pl.ds(base, S), :, WC:].reshape(S * R, WC), w[m * 2 + 1, at, :]
                )
                dp[pl.ds(base, S), :, at] = total.astype(BF16).reshape(S, R, DS // 2)
                rowed = xall[pl.ds(base, S), :, at].reshape(S * R, DS // 2).astype(F32)
                gacc[m, :, at] += jnp.sum(total * rowed, axis=0, keepdims=True)

            @pl.when(j < S)
            def _():
                push(
                    dp.at[pl.ds(base, S)], dr.at[pl.ds((m * (S - 1) + j - 1) * S, S)],
                    send.at[8], d1.at[m * S + j], along_b(m, j),
                ).start()

        for i in range(GR):
            g_core[m * 2 + core, i:i + 1, :] = gacc[m, :, i * 128:(i + 1) * 128]
        mine = g_core.at[m * 2 + core]
        push(mine, mine, send.at[9], s1.at[m], partner).start()

    def weight_grad(m):
        @pl.loop(0, ZL)
        def _(zq):
            at = pl.ds(pl.multiple_of(zq * CH, CH), CH)
            left = xall[pl.ds(m * S * S, S * S), :, at].reshape(S * S * R, CH)
            for half in range(2):
                right = gall[pl.ds(m * S * S, S * S), :, half * WC:(half + 1) * WC]
                work[:, half * WC:(half + 1) * WC] = dot_tn(left, right.reshape(S * S * R, WC))
            upper, lower = work[:WR, :WC], work[WR:, WC:]
            cross = (work[:WR, WC:], work[WR:, :WC])
            first = jnp.where(m == 0, cross[0], cross[1])
            second = jnp.where(m == 0, cross[1], cross[0])
            low = core == 0
            dw_own[m * NZ + zq] = jnp.where(low, upper, first)
            dw_own[m * NZ + ZL + zq] = jnp.where(low, second, lower)
            dw_peer[m * NZ + zq] = jnp.where(low, first, upper).astype(BF16)
            dw_peer[m * NZ + ZL + zq] = jnp.where(low, lower, second).astype(BF16)
            for part in range(2):
                at = m * NZ + part * ZL + zq
                push(dw_peer.at[at], dw_sum.at[at], send.at[10], e1.at[at], partner).start()

    def weight_shares(m):
        @pl.loop(1, NZ + 1)
        def _(k):
            to = lax.rem(z + k, NZ)
            at = m * NZ + to
            arrived(dw_sum.at[at], e1.at[at])
            total = dw_own[at] + dw_sum[at].astype(F32)
            dw_own[at] = total

            @pl.when(k < NZ)
            def _():
                dw_sum[at] = total.astype(BF16)
                push(
                    dw_sum.at[at], dw_z.at[m * (NZ - 1) + k - 1], send.at[11],
                    e2.at[m * NZ + k], along_z(k),
                ).start()

    def gain_step(m, came, slots, going, place_at):
        total = came[m * slots]
        for i in range(1, slots):
            total = total + came[m * slots + i]
        going[place_at] = total

    def gains_b():
        @pl.loop(0, 2)
        def _(m):
            arrived(g_core.at[m * 2 + 1 - core], s1.at[m])
            gain_step(m, g_core, 2, g_b, m * S + bc(m))
            mine = g_b.at[m * S + bc(m)]

            @pl.loop(1, S)
            def _(j):
                push(mine, mine, send.at[12], s2.at[m * S + j], along_b(m, j)).start()

    def gains_z():
        @pl.loop(0, 2)
        def _(m):
            @pl.loop(1, S)
            def _(j):
                arrived(g_b.at[m * S + lax.rem(bc(m) + S - j, S)], s2.at[m * S + j])

            gain_step(m, g_b, S, g_z, m * NZ + z)
            mine = g_z.at[m * NZ + z]

            @pl.loop(1, NZ)
            def _(k):
                push(mine, mine, send.at[13], s3.at[m * NZ + k], along_z(k)).start()

    def gains_c():
        @pl.loop(0, 2)
        def _(m):
            @pl.loop(1, NZ)
            def _(k):
                arrived(g_z.at[m * NZ + lax.rem(z + NZ - k, NZ)], s3.at[m * NZ + k])

            gain_step(m, g_z, NZ, g_c, m * S + cc(m))
            mine = g_c.at[m * S + cc(m)]

            @pl.loop(1, S)
            def _(k):
                push(mine, mine, send.at[14], s4.at[m * S + k], along_c(m, k)).start()

    @pl.loop(0, 2)
    def _(m):
        weight_grad(m)

    gains_b()

    @pl.loop(0, 2)
    def _(m):
        weight_shares(m)

    @pl.loop(0, 2)
    def _(m):
        @pl.loop(1, S + 1)
        def _(j):
            b = lax.rem(bc(m) + j, S)
            mine = (m * S + b) * S + cc(m)
            total = qp[mine].astype(F32)
            for k in range(1, S):
                at = (m * (S - 1) + k - 1) * S + b
                arrived(qr.at[at], q1.at[(m * S + k) * S + b])
                total = total + qr[at].astype(F32)
            qp[mine] = total.astype(BF16)

            @pl.when(j < S)
            def _():
                push(
                    qp.at[mine], qf.at[m * S + bc(m)], send.at[15], q2.at[m * S + j], along_b(m, j)
                ).start()

            @pl.when(j == S)
            def _():
                qf[m * S + bc(m)] = qp[mine]

    gains_z()

    @pl.loop(0, 2)
    def _(m):
        @pl.loop(1, S)
        def _(j):
            arrived(dr.at[pl.ds((m * (S - 1) + j - 1) * S, S)], d1.at[m * S + j])

        @pl.loop(1, S + 1)
        def _(k):
            c = lax.rem(cc(m) + k, S)
            mine = (m * S + bc(m)) * S + c
            total = dp[mine].astype(F32)
            for j in range(1, S):
                total = total + dr[(m * (S - 1) + j - 1) * S + c].astype(F32)
            dp[mine] = total.astype(BF16)

            @pl.when(k < S)
            def _():
                push(
                    dp.at[mine], df.at[m * S + cc(m)], send.at[16], d2.at[m * S + k], along_c(m, k)
                ).start()

            @pl.when(k == S)
            def _():
                df[m * S + cc(m)] = dp[mine]

    gains_c()

    @pl.loop(0, 2)
    def _(m):
        @pl.loop(1, S)
        def _(j):
            arrived(qf.at[m * S + lax.rem(bc(m) + S - j, S)], q2.at[m * S + j])

    @pl.loop(0, S)
    def _(b):
        both = dot_nn(place[0], qf[b]) + dot_nn(place[1], qf[S + b])
        q_out[:, pl.ds(pl.multiple_of(b * ES, ES), ES)] = both.astype(BF16)

    @pl.loop(0, 2)
    def _(m):
        @pl.loop(1, S)
        def _(k):
            arrived(df.at[m * S + lax.rem(cc(m) + S - k, S)], d2.at[m * S + k])

    def columns(i):
        c, zq = lax.div(i, ZL), lax.rem(i, ZL)
        at = pl.ds(pl.multiple_of(zq * (S * CH) + c * CH, CH), CH)
        return c, pl.ds(pl.multiple_of(zq * CH, CH), CH), at

    def scaled(i, along):
        c, local, at = columns(i)
        normed_grad = dot_nn(place[0], df[c, :, local]) + dot_nn(place[1], df[S + c, :, local])
        gains = jnp.where(flag[...] > 0.5, gt_ref[:, at], gi_ref[:, at])
        return normed_grad * gains, tok_ref[:, at].astype(F32) * inv[...], at

    def dots(i, along):
        grads, unit, _ = scaled(i, along)
        return along + jnp.sum(grads * unit, axis=1, keepdims=True)

    along = lax.fori_loop(0, S * ZL, dots, jnp.zeros((T, 1), F32)) / D

    @pl.loop(0, S * ZL)
    def _(i):
        grads, unit, at = scaled(i, along)
        tg_out[:, at] = (inv[...] * (grads - unit * along)).astype(BF16)

    for m, out in ((0, dwt_out), (1, dwi_out)):
        total = dw_own[m * NZ + z]
        for k in range(1, NZ):
            at = m * (NZ - 1) + k - 1
            arrived(dw_z.at[at], e2.at[m * NZ + k])
            total = total + dw_z[at].astype(F32)
        out[...] = total

    for m, out, gain in ((0, ggt_out, gt_ref), (1, ggi_out, gi_ref)):
        @pl.loop(1, S)
        def _(k):
            arrived(g_c.at[m * S + lax.rem(cc(m) + S - k, S)], s4.at[m * S + k])

        for c in range(S):
            for i in range(GR):
                zq, off = (i * 128) // CH, (i * 128) % CH
                at = slice(zq * S * CH + c * CH + off, zq * S * CH + c * CH + off + 128)
                out[:, at] = g_c[m * S + c, i:i + 1, :] / gain[:, at]

    for m in range(2):
        sent(w.at[2 * m], send.at[17 + m])
        sent(w.at[2 * m + 1, pl.ds(0, (NZ - 1) * WR), :], send.at[19 + m])
    sent(gs.at[pl.ds(0, 2 * (S - 1))], send.at[2])
    sent(gall.at[pl.ds(0, 2 * S * (S - 1))], send.at[3])
    sent(xs.at[pl.ds(0, 2 * (S - 1))], send.at[4])
    sent(xall.at[pl.ds(0, 2 * S * (S - 1))], send.at[5])
    sent(qp.at[pl.ds(0, 2 * S * (S - 1))], send.at[7])
    sent(dp.at[pl.ds(0, 2 * S * (S - 1))], send.at[8])
    sent(g_core.at[pl.ds(0, 2)], send.at[9])
    sent(dw_peer, send.at[10])
    sent(dw_sum.at[pl.ds(0, 2 * (NZ - 1))], send.at[11])
    sent(g_b.at[pl.ds(0, 2 * (S - 1))], send.at[12])
    sent(g_z.at[pl.ds(0, 2 * (NZ - 1))], send.at[13])
    sent(g_c.at[pl.ds(0, 2 * (S - 1))], send.at[14])
    sent(qp.at[pl.ds(0, 2 * (S - 1))], send.at[15])
    sent(dp.at[pl.ds(0, 2 * (S - 1))], send.at[16])


def solution(mesh):
    ZL, S = mesh.shape["dp"], mesh.shape["text"] // 2
    NZ = 2 * ZL

    def shards(tokens, modality, gain_text, gain_image, text_weight, image_weight, cotangent):
        T, D = tokens.shape
        E = cotangent.shape[1]
        R = -(-min(CAP, T) // 16) * 16
        DS, ES = D // S, E // S
        CH = DS // ZL
        WR, WC = CH // 2, ES // 2
        GR = DS // 128
        vmem = pl.BlockSpec(memory_space=pltpu.VMEM)
        dma = pltpu.SemaphoreType.DMA
        outs = pl.pallas_call(
            functools.partial(layer, (S, ZL, T, R, DS, ES)),
            out_shape=(
                jax.ShapeDtypeStruct((T, E), BF16),
                jax.ShapeDtypeStruct((T, D), BF16),
                jax.ShapeDtypeStruct((WR, WC), F32),
                jax.ShapeDtypeStruct((WR, WC), F32),
                jax.ShapeDtypeStruct((1, D), F32),
                jax.ShapeDtypeStruct((1, D), F32),
            ),
            in_specs=[vmem] * 7,
            out_specs=(vmem,) * 6,
            scratch_shapes=[
                pltpu.VMEM((2, R, T), BF16),
                pltpu.VMEM((2, T, R), BF16),
                pltpu.VMEM((T, 1), F32),
                pltpu.VMEM((T, 1), F32),
                pltpu.VMEM((CH, ES), F32),
                pltpu.VMEM((2, 1, DS), F32),
                pltpu.VMEM((2 * S, R, DS), BF16),
                pltpu.VMEM((2 * S, R, ES), BF16),
                pltpu.VMEM((2 * S * S, R, DS), BF16),
                pltpu.VMEM((2 * S * S, R, ES), BF16),
                pltpu.VMEM((4, DS, WC), BF16),
                pltpu.VMEM((2 * S * S, R, ES), BF16),
                pltpu.VMEM((2 * S * S, R, DS), BF16),
                pltpu.VMEM((2 * (S - 1) * S, R, ES), BF16),
                pltpu.VMEM((2 * (S - 1) * S, R, DS), BF16),
                pltpu.VMEM((2 * S, R, ES), BF16),
                pltpu.VMEM((2 * S, R, DS), BF16),
                pltpu.VMEM((2 * NZ, WR, WC), F32),
                pltpu.VMEM((2 * NZ, WR, WC), BF16),
                pltpu.VMEM((2 * NZ, WR, WC), BF16),
                pltpu.VMEM((2 * (NZ - 1), WR, WC), BF16),
                pltpu.VMEM((4, GR, 128), F32),
                pltpu.VMEM((2 * S, GR, 128), F32),
                pltpu.VMEM((2 * NZ, GR, 128), F32),
                pltpu.VMEM((2 * S, GR, 128), F32),
                dma((21,)),
                dma((2 * S,)),
                dma((2 * S * S,)),
                dma((2 * S,)),
                dma((2 * S * S,)),
                dma((2 * NZ,)),
                dma((2 * NZ,)),
                dma((2 * S * S,)),
                dma((2 * S,)),
                dma((2 * S,)),
                dma((2 * S,)),
                dma((2 * NZ,)),
                dma((2 * NZ,)),
                dma((2,)),
                dma((2 * S,)),
                dma((2 * NZ,)),
                dma((2 * S,)),
            ],
            compiler_params=pltpu.CompilerParams(
                collective_id=0, has_side_effects=True, vmem_limit_bytes=60 * 2**20
            ),
        )(
            modality.reshape(1, T), gain_text.reshape(1, D), gain_image.reshape(1, D),
            tokens, cotangent, text_weight, image_weight,
        )
        return (*outs[:4], outs[4].reshape(D), outs[5].reshape(D))

    rows = P(("dp", "text", "image"), None)
    text_at, image_at = P(("dp", "image"), "text"), P(("dp", "text"), "image")
    return jax.shard_map(
        shards,
        mesh=mesh,
        in_specs=(rows, P(("dp", "text", "image")), P(), P(), text_at, image_at, rows),
        out_specs=(rows, rows, text_at, image_at, P(), P()),
        check_vma=False,
    )
```

time: 1350 us -> 177 us (0.13)
  waiting for transfers between devices: 1050 us -> 0 us
  blocking collectives: 201 us -> 0 us
  Pallas kernels: 0 us -> 170 us
  matrix products: 43.5 us -> 0 us
  other arithmetic: 19.9 us -> 0 us
  between operations: 15 us -> 0.66 us
    reduce_scatter x4 -> x0, waiting for transfers between devices: 636 us -> none  [the longest x1 301 us: shards(): lax.psum_scatter(weight_term(text_rows, text_grad_cols), ('dp', 'image'),...]
    all_gather x4 -> x0, waiting for transfers between devices: 404 us -> none  [the longest x1 228 us: shards(): lax.all_gather(text_weight, ('dp', 'image'), axis=0, tiled=True)]
    pallas_call x0 -> x1, Pallas kernels: none -> 170 us  [shards(): pl.pallas_call(functools.partial(layer, (S, ZL, T, R, DS, ES)), out_shape...]
    psum x1 -> x0, blocking collectives: 150 us -> none  [shards(): gain_grads = lax.psum((text_term, image_term), ('dp', 'text', 'image'))]
    all_to_all x2 -> x0, blocking collectives: 51.1 us -> none  [the longest x1 36.7 us: shards(): lax.all_to_all(image_up, 'image', split_axis=1, concat_axis=0, tiled=True)]
    dot_general x6 -> x0, matrix products: 43.5 us -> none  [the longest x2 16.2 us: weight_term(): lax.dot_general(left_rows, upstream, (((0,), (0,)), ((), ())), preferred_...]
  transfers between devices with their start and end apart: 10 -> 0, of which waited for: 9 -> 0; matrix products, arithmetic and copies ran while one was open for 5% -> 0% of each run, Pallas kernels for 0% -> 0%
where the time goes in v1:
time: 177 us
  Pallas kernels  170 us (96%)
  local copies, waits for them, and re-layouts  6.56 us (4%)
    pallas_call x1, Pallas kernels, shards(): pl.pallas_call(functools.partial(layer, (S, ZL, T, R, DS, ES)), out_shape...  170 us
    unnamed x16, local copies, waits for them, and re-layouts  6.56 us

profile of v1, /device:TPU:2, one launch (start us, length us, event | category | flops | bytes accessed | tf_op | source)
XLA Modules:
  0.0 176.9 jit_solution(9140046168717690900)
XLA Ops:
  0.6 169.7 %shard_map.118 = (bf16[128,4096]{1,0:T(8,128)(2,1)}, bf16[128,4096]{1,0:T(8,128)(2,1)}, f32[128,512]{1,0:T(8,128)}, f32[128,512]{1,0:T(8,128)}, f32[1,4096]{1,0:T(1,128)}, /*index=5*/f32[1,4096]{1,0:T(1,128)}) custom-call(s32[1,128]{1,0:T(1,128)} %bitcast.9, f32[1,4096]{1,0:T(1,128)} %bitcast.5, f32[1,4096]{1,0:T(1,128)} %bitcast.6, ...), custom_call_target="tpu_custom_call" | custom-call | tf_op jit(solution)/shard_map/pallas_call | solution.py:526
  170.3 0.0 copy-start
  170.4 2.4 %copy.19 = bf16[128,4096]{1,0:T(8,128)(2,1)} copy(bf16[128,4096]{1,0:T(8,128)(2,1)} %get-tuple-element.24) | data formatting | bytes 2097152
  172.7 0.0 copy-done
  172.7 0.0 copy-start.2
  172.7 1.0 copy.20
  173.7 0.1 copy-done.2
  173.8 0.0 copy-start.1
  173.8 0.7 copy.21
  174.5 0.3 copy-done.1
  174.9 0.0 copy-start.4
  174.9 0.7 copy.22
  175.6 0.0 copy-done.4
  175.6 0.0 copy-start.3
  175.6 0.6 copy.23
  176.2 0.1 copy-done.3
  176.3 0.6 copy.24
Async XLA Ops:
  170.3 2.4 %copy-start = (bf16[128,4096]{1,0:T(8,128)(2,1)S(1)}, bf16[128,4096]{1,0:T(8,128)(2,1)}, u32[]{:S(2)}) copy-start(bf16[128,4096]{1,0:T(8,128)(2,1)} %get-tuple-element.25) | copy-start | bytes 3145732
  172.7 1.1 copy-start.2
  173.8 1.0 copy-start.1
  174.9 0.7 copy-start.4
  175.6 0.7 copy-start.3

commit v2 on v0

v2 whole, which is shorter than its diff:
```python
import functools

import jax
import jax.numpy as jnp
from jax import lax
from jax.experimental import pallas as pl
from jax.experimental.pallas import tpu as pltpu
from jax.sharding import PartitionSpec as P

MESH = pl.DeviceIdType.MESH
CAP = 72
EPSILON = 1e-05
F32 = jnp.float32
BF16 = jnp.bfloat16


def dot_nn(left, right):
    return jnp.dot(left, right, preferred_element_type=F32)


def dot_nt(left, right):
    return lax.dot_general(left, right, (((1,), (1,)), ((), ())), preferred_element_type=F32)


def dot_tn(left, right):
    return lax.dot_general(left, right, (((0,), (0,)), ((), ())), preferred_element_type=F32)


def ranks(modality, T):
    rows = lax.broadcasted_iota(jnp.int32, (T, T), 0)
    cols = lax.broadcasted_iota(jnp.int32, (T, T), 1)
    flag_row = jnp.where(modality == 0, 1.0, 0.0)
    wide = jnp.broadcast_to(flag_row, (T, T))
    flag_col = jnp.sum(jnp.where(rows == cols, wide, 0.0), axis=1, keepdims=True)
    rank_col = jnp.sum(jnp.where(cols < rows, wide, 0.0), axis=1, keepdims=True)
    tall = jnp.broadcast_to(flag_col, (T, T))
    rank_row = jnp.sum(jnp.where(rows < cols, tall, 0.0), axis=0, keepdims=True)
    return flag_row, flag_col, rank_row, rank_col


def layer(
    dims,
    mod_ref, gt_ref, gi_ref, tok_in, cot_in, wt_in, wi_in,
    qf_out, df_out, dw_out, dwx_out, gain_out,
    tok_ref, cot_ref, pick, flag, inv, work, gacc,
    xs, gs, xall, gall, w, qp, dp, qr, dm, dr, qf, df,
    dw_own, dw_peer, dw_sum, ring, dw_x, dw_xr, dw_end,
    g_core, g_b, g_z, g_c,
    local, send, x1, x2, g1, g2, wx, w1, w2, q1, q2, d0, d1, d2, e1, e2, e3, s1, s2, s3, s4,
):
    S, ZL, T, R, DS, ES = dims
    NZ = 2 * ZL
    H = NZ // 2
    CH = DS // ZL
    WR, WC = CH // 2, ES // 2
    WH = WR // 2
    D, E = DS * S, ES * S
    GR = DS // 128
    zl, text, image = lax.axis_index("dp"), lax.axis_index("text"), lax.axis_index("image")
    y, core = lax.div(text, 2), lax.rem(text, 2)
    x, zh = lax.div(image, 2), lax.rem(image, 2)
    z = zh * ZL + zl

    def cc(m):
        return x + (y - x) * m

    def bc(m):
        return y + (x - y) * m

    def odd(m):
        return lax.rem(cc(m), 2)

    def along_c(m, k):
        return (zl, lax.rem(text + 2 * k * m, 2 * S), lax.rem(image + 2 * k * (1 - m), 2 * S))

    def along_b(m, k):
        return (zl, lax.rem(text + 2 * k * (1 - m), 2 * S), lax.rem(image + 2 * k * m, 2 * S))

    def along_z(k):
        to = lax.rem(z + k, NZ)
        return (lax.rem(to, ZL), text, 2 * x + lax.div(to, ZL))

    def mate(m):
        return along_c(m, 1 + (S - 2) * lax.rem(cc(m) + core, 2))

    def twin(m):
        return along_c(m, 2)

    partner = (zl, text + 1 - 2 * core, image)

    def push(src, dst, send_sem, recv_sem, device):
        return pltpu.make_async_remote_copy(
            src_ref=src, dst_ref=dst, send_sem=send_sem, recv_sem=recv_sem,
            device_id=device, device_id_type=MESH,
        )

    def arrived(dst, recv_sem):
        push(dst, dst, send.at[21], recv_sem, partner).wait_recv()

    def sent(src, send_sem):
        push(src, src, send_sem, q1.at[0], partner).wait_send()

    barrier = pltpu.get_barrier_semaphore()

    @pl.loop(1, S)
    def _(k):
        pl.semaphore_signal(barrier, inc=1, device_id=along_c(0, k), device_id_type=MESH)
        pl.semaphore_signal(barrier, inc=1, device_id=along_b(0, k), device_id_type=MESH)

    @pl.loop(1, NZ)
    def _(k):
        pl.semaphore_signal(barrier, inc=1, device_id=along_z(k), device_id_type=MESH)

    pl.semaphore_signal(barrier, inc=1, device_id=partner, device_id_type=MESH)

    flag_row, flag_col, rank_row, _ = ranks(mod_ref[...], T)
    flag[...] = flag_col
    slot = lax.broadcasted_iota(jnp.int32, (R, T), 0).astype(F32)
    spot = lax.broadcasted_iota(jnp.int32, (R, T), 1).astype(F32)
    pick[:R] = jnp.where((rank_row == slot) & (flag_row > 0.5), 1.0, 0.0).astype(BF16)
    pick[R:] = jnp.where((spot - rank_row == slot) & (flag_row < 0.5), 1.0, 0.0).astype(BF16)

    def w_at(m, g, from_z, from_core, part=None):
        from_zh, from_zl = lax.div(from_z, ZL), lax.rem(from_z, ZL)
        half = from_core + (from_zh - from_core) * m
        row = 2 * from_zl + from_zh + (from_core - from_zh) * m
        if part is None:
            at = pl.ds(pl.multiple_of(row * WR, WR), WR)
        else:
            at = pl.ds(pl.multiple_of(row * WR + part * WH, WH), WH)
        return w.at[(m * 2 + g) * 2 + half, at, :]

    def group(m):
        return lax.div(cc(m), 2)

    loads = [
        pltpu.make_async_copy(wt_in, w_at(0, group(0), z, core), local.at[0]),
        pltpu.make_async_copy(wi_in, w_at(1, group(1), z, core), local.at[1]),
        pltpu.make_async_copy(cot_in, cot_ref, local.at[2]),
        pltpu.make_async_copy(tok_in, tok_ref, local.at[3]),
    ]
    for load in loads:
        load.start()

    def ring_w(t, m, g):
        lane = m * 2 + g
        if t < H:
            for way, step in ((0, 1), (1, NZ - 1)):
                block = w_at(m, g, lax.rem(z + (NZ - step) * (t - 1), NZ), core)
                push(block, block, send.at[18], w1.at[(way * H + t - 1) * 4 + lane], along_z(step)).start()
        else:
            for way, step in ((0, 1), (1, NZ - 1)):
                block = w_at(m, g, lax.rem(z + (NZ - step) * (t - 1), NZ), core, way)
                push(block, block, send.at[19], w1.at[(way * H + t - 1) * 4 + lane], along_z(step)).start()

    def ring_w_came(t, m, g):
        lane = m * 2 + g
        for way, step in ((0, 1), (1, NZ - 1)):
            origin = lax.rem(z + (NZ - step) * t, NZ)
            if t < H:
                block = w_at(m, g, origin, core)
                arrived(block, w1.at[(way * H + t - 1) * 4 + lane])
                push(block, block, send.at[1], w2.at[lane * NZ + origin], partner).start()
            else:
                arrived(w_at(m, g, origin, core, way), w1.at[(way * H + t - 1) * 4 + lane])
        if t == H:
            block = w_at(m, g, lax.rem(z + H, NZ), core)
            push(block, block, send.at[1], w2.at[lane * NZ + lax.rem(z + H, NZ)], partner).start()

    loads[0].wait()
    loads[1].wait()
    pl.semaphore_wait(barrier, 2 * (S - 1) + NZ)

    @pl.loop(0, 2)
    def _(m):
        mine = w_at(m, group(m), z, core)
        push(mine, mine, send.at[17], wx.at[m], twin(m)).start()
        ring_w(1, m, group(m))
        push(mine, mine, send.at[1], w2.at[(m * 2 + group(m)) * NZ + z], partner).start()

    loads[2].wait()

    @pl.loop(0, S)
    def _(b):
        part = cot_ref[:, pl.ds(pl.multiple_of(b * ES, ES), ES)]
        chosen = dot_nn(pick[...], part).astype(BF16)
        gs[b] = chosen[:R]
        gs[S + b] = chosen[R:]

    def token_rows(m, b, p):
        return (m * S + b) * 2 + p

    @pl.loop(0, 2)
    def _(m):
        mine = token_rows(m, bc(m), odd(m))
        gall[mine] = gs[m * S + bc(m)]

        @pl.loop(1, S)
        def _(j):
            to = lax.rem(bc(m) + j, S)
            push(gs.at[m * S + to], gall.at[mine], send.at[2], g1.at[m * S + j], along_b(m, j)).start()

        push(gall.at[mine], gall.at[mine], send.at[3], g2.at[m * S], mate(m)).start()

    loads[3].wait()
    squares = jnp.zeros((T, CH), F32)
    for i in range(S * ZL):
        part = tok_ref[:, i * CH:(i + 1) * CH].astype(F32)
        squares = squares + part * part
    inv[...] = lax.rsqrt(jnp.sum(squares, axis=1, keepdims=True) / D + EPSILON)

    @pl.loop(0, S * ZL)
    def _(i):
        c, zq = lax.div(i, ZL), lax.rem(i, ZL)
        at = pl.ds(pl.multiple_of(zq * (S * CH) + c * CH, CH), CH)
        to = pl.ds(pl.multiple_of(zq * CH, CH), CH)
        unit = tok_ref[:, at].astype(F32) * inv[...]
        gains = jnp.where(flag[...] > 0.5, gt_ref[:, at], gi_ref[:, at])
        normed = (unit * gains).astype(BF16)
        half, g = lax.rem(c, 2), lax.div(c, 2)
        chosen = dot_nn(pick[...], normed).astype(BF16)
        xs[half, g, :, to] = chosen[:R]
        xs[2 + half, g, :, to] = chosen[R:]

    def spread(m, kind):
        block = xall.at[token_rows(m, bc(m), odd(m) + kind - 2 * odd(m) * kind)]
        for way, step in ((0, 1), (1, S - 1)):
            push(block, block, send.at[5], x2.at[(m * 2 + kind) * 4 + way], along_b(m, step)).start()

    def spread_on(m, kind):
        p = odd(m) + kind - 2 * odd(m) * kind
        for way, step in ((0, 1), (1, S - 1)):
            block = xall.at[token_rows(m, lax.rem(bc(m) + S - step, S), p)]
            arrived(block, x2.at[(m * 2 + kind) * 4 + way])
            push(
                block.at[way], block.at[way], send.at[0], x2.at[(m * 2 + kind) * 4 + 2 + way],
                along_b(m, step),
            ).start()

    def spread_end(m, kind):
        p = odd(m) + kind - 2 * odd(m) * kind
        block = xall.at[token_rows(m, lax.rem(bc(m) + 2, S), p)]
        for way in range(2):
            arrived(block.at[way], x2.at[(m * 2 + kind) * 4 + 2 + way])

    def both(step, *rest):
        @pl.loop(0, 2)
        def _(m):
            step(m, *rest)

    @pl.loop(0, 2)
    def _(m):
        mine = token_rows(m, bc(m), odd(m))
        push(xs.at[m * 2 + 1 - odd(m)], xall.at[mine], send.at[4], x1.at[m], mate(m)).start()
        xall[mine] = xs[m * 2 + odd(m)]
        spread(m, 0)

    @pl.loop(0, 2)
    def _(m):
        other = 1 - group(m)
        block = w_at(m, other, z, core)
        arrived(block, wx.at[m])
        ring_w(1, m, other)
        push(block, block, send.at[1], w2.at[(m * 2 + other) * NZ + z], partner).start()

    def pass_on_grads(j):
        @pl.loop(0, 2)
        def _(m):
            block = gall.at[token_rows(m, lax.rem(bc(m) + S - j, S), odd(m))]
            arrived(block, g1.at[m * S + j])
            push(block, block, send.at[3], g2.at[m * S + j], mate(m)).start()

    def ring_w_on(t, kind):
        @pl.loop(0, 2)
        def _(m):
            g = group(m) + kind - 2 * group(m) * kind
            ring_w_came(t, m, g)
            if t < H:
                ring_w(t + 1, m, g)

    @pl.loop(0, 2)
    def _(m):
        arrived(xall.at[token_rows(m, bc(m), 1 - odd(m))], x1.at[m])
        spread(m, 1)

    pass_on_grads(1)
    ring_w_on(1, 0)
    pass_on_grads(3)
    pass_on_grads(2)
    ring_w_on(1, 1)
    both(spread_on, 0)
    if H > 1:
        ring_w_on(2, 0)
        ring_w_on(2, 1)
    both(spread_on, 1)
    for t in range(3, H + 1):
        ring_w_on(t, 0)
        ring_w_on(t, 1)
    both(spread_end, 0)
    both(spread_end, 1)

    @pl.loop(0, 2)
    def _(m):
        @pl.loop(0, S)
        def _(j):
            b = lax.rem(bc(m) + S - j, S)
            arrived(gall.at[token_rows(m, b, 1 - odd(m))], g2.at[m * S + j])

    def weight_grad(lane):
        m, g = lane // 2, lane % 2

        @pl.loop(0, ZL)
        def _(zq):
            at = pl.ds(pl.multiple_of(zq * CH, CH), CH)
            left = xall[pl.ds(m * 2 * S, 2 * S), g, :, at].reshape(2 * S * R, CH)
            for half in range(2):
                right = gall[pl.ds(m * 2 * S, 2 * S), :, half * WC:(half + 1) * WC]
                work[:, half * WC:(half + 1) * WC] = dot_tn(left, right.reshape(2 * S * R, WC))
            upper, lower = work[:WR, :WC], work[WR:, WC:]
            cross = (work[:WR, WC:], work[WR:, :WC])
            first, second = cross[m], cross[1 - m]
            low = core == 0
            dw_own[lane * NZ + zq] = jnp.where(low, upper, first).astype(BF16)
            dw_own[lane * NZ + ZL + zq] = jnp.where(low, second, lower).astype(BF16)
            dw_peer[lane * NZ + zq] = jnp.where(low, first, upper).astype(BF16)
            dw_peer[lane * NZ + ZL + zq] = jnp.where(low, lower, second).astype(BF16)
            for part in range(2):
                to = lane * NZ + part * ZL + zq
                push(dw_peer.at[to], dw_sum.at[to], send.at[10], e1.at[to], partner).start()

    def share(lane, to):
        return dw_own[lane * NZ + to].astype(F32) + dw_sum[lane * NZ + to].astype(F32)

    def ring_start(lane):
        to = lax.rem(z + H, NZ)
        at = lane * NZ + to
        arrived(dw_sum.at[at], e1.at[at])
        dw_own[at] = share(lane, to).astype(BF16)
        for way, step in ((0, 1), (1, NZ - 1)):
            half = pl.ds(way * WH, WH)
            push(
                dw_own.at[at, half], ring.at[(way * H) * 4 + lane, half], send.at[6],
                e2.at[(way * H) * 4 + lane], along_z(step),
            ).start()

    def ring_step(t, lane):
        for way, step in ((0, 1), (1, NZ - 1)):
            to = lax.rem(z + step * (H - t), NZ)
            at = (way * H + t - 1) * 4 + lane
            arrived(dw_sum.at[lane * NZ + to], e1.at[lane * NZ + to])
            own = share(lane, to)
            if t == 1:
                half, rest = pl.ds(way * WH, WH), pl.ds((1 - way) * WH, WH)
                arrived(ring.at[at, half], e2.at[at])
                total = ring[at, half].astype(F32) + own[way * WH:(way + 1) * WH]
                ring[at, half] = total.astype(BF16)
                ring[at, rest] = own[(1 - way) * WH:(2 - way) * WH].astype(BF16)
            else:
                arrived(ring.at[at], e2.at[at])
                ring[at] = (ring[at].astype(F32) + own).astype(BF16)
            push(ring.at[at], ring.at[at + 4], send.at[11], e2.at[at + 4], along_z(step)).start()

    def ring_end(lane):
        arrived(dw_sum.at[lane * NZ + z], e1.at[lane * NZ + z])
        total = share(lane, z)
        for way in range(2):
            at = (way * H + H - 1) * 4 + lane
            if H == 1:
                half, rest = pl.ds(way * WH, WH), pl.ds((1 - way) * WH, WH)
                arrived(ring.at[at, half], e2.at[at])
                ring[at, rest] = jnp.zeros((WH, WC), BF16)
            else:
                arrived(ring.at[at], e2.at[at])
            total = total + ring[at].astype(F32)
        return total

    def queries(m):
        @pl.loop(0, S // 2)
        def _(i):
            base = token_rows(m, 2 * i, 0)
            for half in range(2):
                total = jnp.zeros((4 * R, WC), F32)
                for g in range(2):
                    block = xall[pl.ds(base, 4), g].reshape(4 * R, DS)
                    total = total + dot_nn(block, w[(m * 2 + g) * 2 + half])
                qp[pl.ds(base, 4), :, half * WC:(half + 1) * WC] = total.astype(BF16).reshape(4, R, WC)
            for n in range(2):
                b = 2 * i + n
                push(
                    qp.at[token_rows(m, b, 1 - odd(m))], qr.at[m * S + b], send.at[7],
                    q1.at[m * S + b], mate(m),
                ).start()

    def input_grads(m, first, second):
        bases = [token_rows(m, lax.rem(bc(m) + step, S), 0) for step in (first, second)]

        def taken(ref, *at):
            return jnp.concatenate([ref[(pl.ds(base, 2), *at)] for base in bases], axis=0)

        for g in range(2):
            for part in range(2):
                at = slice(part * (DS // 2), (part + 1) * (DS // 2))
                total = dot_nt(
                    taken(gall, slice(None), slice(0, WC)).reshape(4 * R, WC), w[(m * 2 + g) * 2, at, :]
                ) + dot_nt(
                    taken(gall, slice(None), slice(WC, ES)).reshape(4 * R, WC), w[(m * 2 + g) * 2 + 1, at, :]
                )
                short = total.astype(BF16).reshape(4, R, DS // 2)
                dp[pl.ds(bases[0], 2), g, :, at] = short[:2]
                dp[pl.ds(bases[1], 2), g, :, at] = short[2:]
                rowed = taken(xall, g, slice(None), at).reshape(4 * R, DS // 2).astype(F32)
                gacc[m * 2 + g, :, at] += jnp.sum(total * rowed, axis=0, keepdims=True)

    def rows_to(m, step):
        return pl.ds(token_rows(m, lax.rem(bc(m) + step, S), 0), 2)

    def grads_near(m, way, g):
        push(
            dp.at[rows_to(m, (1, S - 1)[way]), g], dr.at[pl.ds((m * 2 + way) * 2, 2), g],
            send.at[8], d1.at[(m * 2 + way) * 2 + g], along_b(m, (1, S - 1)[way]),
        ).start()

    def input_grads_first(m):
        input_grads(m, 2, 1)
        for way in range(2):
            push(
                dp.at[rows_to(m, 2), way], dm.at[pl.ds((m * 2 + way) * 2, 2)],
                send.at[22], d0.at[m * 2 + way], along_b(m, (1, S - 1)[way]),
            ).start()
        grads_near(m, 0, 1)

    def input_grads_last(m):
        input_grads(m, S - 1, 0)
        grads_near(m, 1, 0)

    def input_grads_mid(m):
        for way in range(2):
            came = dm.at[pl.ds((m * 2 + way) * 2, 2)]
            arrived(came, d0.at[m * 2 + way])
            at = rows_to(m, (1, S - 1)[way])
            dp[at, way] = (dp[at, way].astype(F32) + came[...].astype(F32)).astype(BF16)
            grads_near(m, way, way)

    def gain_step(m, came, slots, going, place_at):
        total = came[m * slots]
        for i in range(1, slots):
            total = total + came[m * slots + i]
        going[place_at] = total

    def gains_core():
        @pl.loop(0, 2)
        def _(m):
            for g in range(2):
                for i in range(GR):
                    g_core[m * 2 + core, g * GR + i:g * GR + i + 1, :] = gacc[
                        m * 2 + g, :, i * 128:(i + 1) * 128
                    ]
            mine = g_core.at[m * 2 + core]
            push(mine, mine, send.at[9], s1.at[m], partner).start()

    def gains_b():
        @pl.loop(0, 2)
        def _(m):
            arrived(g_core.at[m * 2 + 1 - core], s1.at[m])
            gain_step(m, g_core, 2, g_b, m * S + bc(m))
            mine = g_b.at[m * S + bc(m)]

            @pl.loop(1, S)
            def _(j):
                push(mine, mine, send.at[12], s2.at[m * S + j], along_b(m, j)).start()

    def gains_z():
        @pl.loop(0, 2)
        def _(m):
            @pl.loop(1, S)
            def _(j):
                arrived(g_b.at[m * S + lax.rem(bc(m) + S - j, S)], s2.at[m * S + j])

            gain_step(m, g_b, S, g_z, m * NZ + z)
            mine = g_z.at[m * NZ + z]

            @pl.loop(1, NZ)
            def _(k):
                push(mine, mine, send.at[13], s3.at[m * NZ + k], along_z(k)).start()

    def gains_c():
        @pl.loop(0, 2)
        def _(m):
            @pl.loop(1, NZ)
            def _(k):
                arrived(g_z.at[m * NZ + lax.rem(z + NZ - k, NZ)], s3.at[m * NZ + k])

            gain_step(m, g_z, NZ, g_c, m * S + cc(m))
            mine = g_c.at[m * S + cc(m)]

            @pl.loop(1, S)
            def _(k):
                push(mine, mine, send.at[14], s4.at[m * S + k], along_c(m, k)).start()

    def query_sums(m):
        @pl.loop(1, S + 1)
        def _(j):
            b = lax.rem(bc(m) + j, S)
            mine = token_rows(m, b, odd(m))
            arrived(qr.at[m * S + b], q1.at[m * S + b])
            total = (qp[mine].astype(F32) + qr[m * S + b].astype(F32)).astype(BF16)

            @pl.when(j < S)
            def _():
                qp[mine] = total
                push(
                    qp.at[mine], qf.at[m * S + bc(m)], send.at[15], q2.at[m * S + j], along_b(m, j)
                ).start()

            @pl.when(j == S)
            def _():
                qf[m * S + bc(m)] = total

    def grad_sums(m):
        for way in range(2):
            for g in range(2):
                arrived(dr.at[pl.ds((m * 2 + way) * 2, 2), g], d1.at[(m * 2 + way) * 2 + g])

        def summed(p, g):
            total = dp[token_rows(m, bc(m), p), g].astype(F32)
            for way in range(2):
                total = total + dr[(m * 2 + way) * 2 + p, g].astype(F32)
            return total.astype(BF16)

        theirs = token_rows(m, bc(m), 1 - odd(m))
        for g in range(2):
            dp[theirs, g] = summed(1 - odd(m), g)
        push(dp.at[theirs], df.at[m * 2 + odd(m)], send.at[16], d2.at[m], mate(m)).start()
        for g in range(2):
            df[m * 2 + odd(m), g] = summed(odd(m), g)

    def steps(t, *lanes):
        if t < H:
            for lane in lanes:
                ring_step(t, lane)

    gacc[...] = jnp.zeros_like(gacc)
    weight_grad(0)

    @pl.loop(0, 4 * NZ)
    def _(i):
        lane, k = lax.div(i, NZ), lax.rem(i, NZ)
        m, g = lax.div(lane, 2), lax.rem(lane, 2)
        arrived(w_at(m, g, k, 1 - core), w2.at[lane * NZ + k])

    both(input_grads_first)
    ring_start(0)
    weight_grad(1)
    ring_start(1)
    steps(1, 0)
    both(input_grads_last)
    gains_core()
    input_grads_mid(0)
    weight_grad(2)
    ring_start(2)
    steps(1, 1)
    input_grads_mid(1)
    weight_grad(3)
    ring_start(3)
    steps(1, 2)
    steps(2, 0)
    queries(0)
    steps(1, 3)
    steps(2, 1)
    queries(1)
    gains_b()
    steps(2, 2, 3)
    query_sums(0)
    steps(3, 0)
    query_sums(1)
    steps(3, 1)
    gains_z()
    grad_sums(0)
    steps(3, 2)
    grad_sums(1)
    steps(3, 3)
    gains_c()

    @pl.loop(0, 2)
    def _(m):
        other = 1 - group(m)
        dw_x[m] = ring_end(m * 2 + other).astype(BF16)
        push(dw_x.at[m], dw_xr.at[m], send.at[20], e3.at[m], twin(m)).start()

    @pl.loop(0, 2)
    def _(m):
        @pl.loop(1, S)
        def _(j):
            arrived(qf.at[m * S + lax.rem(bc(m) + S - j, S)], q2.at[m * S + j])

    stores = [
        pltpu.make_async_copy(qf, qf_out, local.at[0]),
        pltpu.make_async_copy(df, df_out, local.at[1]),
        pltpu.make_async_copy(dw_end, dw_out, local.at[2]),
        pltpu.make_async_copy(dw_xr, dwx_out, local.at[3]),
        pltpu.make_async_copy(g_c, gain_out, local.at[4]),
    ]
    stores[0].start()

    @pl.loop(0, 2)
    def _(m):
        arrived(df.at[m * 2 + 1 - odd(m)], d2.at[m])

    stores[1].start()

    @pl.loop(0, 2)
    def _(m):
        dw_end[m] = ring_end(m * 2 + group(m))

    stores[2].start()

    @pl.loop(0, 2)
    def _(m):
        @pl.loop(1, S)
        def _(k):
            arrived(g_c.at[m * S + lax.rem(cc(m) + S - k, S)], s4.at[m * S + k])

    stores[4].start()

    @pl.loop(0, 2)
    def _(m):
        arrived(dw_xr.at[m], e3.at[m])

    stores[3].start()

    sent(w.at[pl.ds(0, 4)], send.at[1])
    sent(gs.at[pl.ds(0, 2 * (S - 1))], send.at[2])
    sent(gall.at[pl.ds(0, 2 * S)], send.at[3])
    sent(xs.at[pl.ds(0, 2)], send.at[4])
    sent(xall.at[pl.ds(0, 8)], send.at[5])
    sent(xall.at[pl.ds(0, 4)], send.at[0])
    sent(dw_own.at[pl.ds(0, 4)], send.at[6])
    sent(qp.at[pl.ds(0, 2 * S)], send.at[7])
    sent(dp.at[pl.ds(0, 8)], send.at[8])
    sent(dp.at[pl.ds(0, 4)], send.at[22])
    sent(g_core.at[pl.ds(0, 2)], send.at[9])
    sent(dw_peer, send.at[10])
    if H > 1:
        sent(ring.at[pl.ds(0, 8 * (H - 1))], send.at[11])
    sent(g_b.at[pl.ds(0, 2 * (S - 1))], send.at[12])
    sent(g_z.at[pl.ds(0, 2 * (NZ - 1))], send.at[13])
    sent(g_c.at[pl.ds(0, 2 * (S - 1))], send.at[14])
    sent(qp.at[pl.ds(0, 2 * (S - 1))], send.at[15])
    sent(dp.at[pl.ds(0, 2)], send.at[16])
    sent(dw_x, send.at[17])
    if H > 1:
        sent(ring.at[pl.ds(0, 8 * (H - 1))], send.at[18])
    sent(dw_own.at[pl.ds(0, 4)], send.at[19])
    sent(dw_x, send.at[20])
    for store in stores:
        store.wait()


def finish(
    dims,
    mod_ref, gt_ref, gi_ref, tok_ref, qf, df, dw_ref, dwx_ref, gain_ref,
    q_out, tg_out, dwt_out, dwi_out, ggt_out, ggi_out,
    grads,
):
    S, ZL, T, R, DS, ES = dims
    CH = DS // ZL
    GR = DS // 128
    D = DS * S
    _, flag, _, rank_col = ranks(mod_ref[...], T)
    slot = lax.broadcasted_iota(jnp.int32, (T, R), 1).astype(F32)
    spot = lax.broadcasted_iota(jnp.int32, (T, R), 0).astype(F32)
    text = jnp.where((rank_col == slot) & (flag > 0.5), 1.0, 0.0).astype(BF16)
    image = jnp.where((spot - rank_col == slot) & (flag < 0.5), 1.0, 0.0).astype(BF16)

    squares = jnp.zeros((T, CH), F32)
    products = jnp.zeros((T, CH), F32)
    for c in range(S):
        half, g = c % 2, c // 2
        normed_grad = dot_nn(text, df[half, g]) + dot_nn(image, df[2 + half, g])
        for zq in range(ZL):
            at = slice(zq * S * CH + c * CH, zq * S * CH + (c + 1) * CH)
            gains = jnp.where(flag > 0.5, gt_ref[:, at], gi_ref[:, at])
            part = normed_grad[:, zq * CH:(zq + 1) * CH] * gains
            token = tok_ref[:, at].astype(F32)
            grads[:, at] = part
            squares = squares + token * token
            products = products + part * token
    inv = lax.rsqrt(jnp.sum(squares, axis=1, keepdims=True) / D + EPSILON)
    along = jnp.sum(products, axis=1, keepdims=True) / D * inv * inv

    for i in range(S * ZL):
        at = slice(i * CH, (i + 1) * CH)
        tg_out[:, at] = (inv * (grads[:, at] - tok_ref[:, at].astype(F32) * along)).astype(BF16)

    for b in range(S):
        full = dot_nn(text, qf[b]) + dot_nn(image, qf[S + b])
        q_out[:, b * ES:(b + 1) * ES] = full.astype(BF16)

    dwt_out[...] = dw_ref[0] + dwx_ref[0].astype(F32)
    dwi_out[...] = dw_ref[1] + dwx_ref[1].astype(F32)

    for m, out, gain in ((0, ggt_out, gt_ref), (1, ggi_out, gi_ref)):
        for half in range(2):
            total = gain_ref[m * S + half]
            for k in range(half + 2, S, 2):
                total = total + gain_ref[m * S + k]
            for g in range(S // 2):
                for i in range(GR):
                    zq, off = (i * 128) // CH, (i * 128) % CH
                    first = zq * S * CH + (half + 2 * g) * CH + off
                    at = slice(first, first + 128)
                    out[:, at] = total[g * GR + i:g * GR + i + 1, :] / gain[:, at]


def solution(mesh):
    ZL, S = mesh.shape["dp"], mesh.shape["text"] // 2
    NZ = 2 * ZL
    H = NZ // 2

    def shards(tokens, modality, gain_text, gain_image, text_weight, image_weight, cotangent):
        T, D = tokens.shape
        E = cotangent.shape[1]
        R = -(-min(CAP, T) // 16) * 16
        DS, ES = D // S, E // S
        CH = DS // ZL
        WR, WC = CH // 2, ES // 2
        GR = DS // 128
        vmem = pl.BlockSpec(memory_space=pltpu.VMEM)
        dma = pltpu.SemaphoreType.DMA
        dims = (S, ZL, T, R, DS, ES)
        anywhere = pl.BlockSpec(memory_space=pl.ANY)
        modality, gain_text, gain_image = (
            modality.reshape(1, T), gain_text.reshape(1, D), gain_image.reshape(1, D)
        )
        parts = pl.pallas_call(
            functools.partial(layer, dims),
            out_shape=(
                jax.ShapeDtypeStruct((2 * S, R, ES), BF16),
                jax.ShapeDtypeStruct((4, 2, R, DS), BF16),
                jax.ShapeDtypeStruct((2, WR, WC), F32),
                jax.ShapeDtypeStruct((2, WR, WC), BF16),
                jax.ShapeDtypeStruct((2 * S, 2 * GR, 128), F32),
            ),
            in_specs=[vmem] * 3 + [anywhere] * 4,
            out_specs=(anywhere,) * 5,
            scratch_shapes=[
                pltpu.VMEM((T, D), BF16),
                pltpu.VMEM((T, E), BF16),
                pltpu.VMEM((2 * R, T), BF16),
                pltpu.VMEM((T, 1), F32),
                pltpu.VMEM((T, 1), F32),
                pltpu.VMEM((CH, ES), F32),
                pltpu.VMEM((4, 1, DS), F32),
                pltpu.VMEM((4, 2, R, DS), BF16),
                pltpu.VMEM((2 * S, R, ES), BF16),
                pltpu.VMEM((4 * S, 2, R, DS), BF16),
                pltpu.VMEM((4 * S, R, ES), BF16),
                pltpu.VMEM((8, DS, WC), BF16),
                pltpu.VMEM((4 * S, R, ES), BF16),
                pltpu.VMEM((4 * S, 2, R, DS), BF16),
                pltpu.VMEM((2 * S, R, ES), BF16),
                pltpu.VMEM((8, R, DS), BF16),
                pltpu.VMEM((8, 2, R, DS), BF16),
                pltpu.VMEM((2 * S, R, ES), BF16),
                pltpu.VMEM((4, 2, R, DS), BF16),
                pltpu.VMEM((4 * NZ, WR, WC), BF16),
                pltpu.VMEM((4 * NZ, WR, WC), BF16),
                pltpu.VMEM((4 * NZ, WR, WC), BF16),
                pltpu.VMEM((8 * H, WR, WC), BF16),
                pltpu.VMEM((2, WR, WC), BF16),
                pltpu.VMEM((2, WR, WC), BF16),
                pltpu.VMEM((2, WR, WC), F32),
                pltpu.VMEM((4, 2 * GR, 128), F32),
                pltpu.VMEM((2 * S, 2 * GR, 128), F32),
                pltpu.VMEM((2 * NZ, 2 * GR, 128), F32),
                pltpu.VMEM((2 * S, 2 * GR, 128), F32),
                dma((5,)),
                dma((23,)),
                dma((2,)),
                dma((16,)),
                dma((2 * S,)),
                dma((2 * S,)),
                dma((2,)),
                dma((8 * H,)),
                dma((4 * NZ,)),
                dma((2 * S,)),
                dma((2 * S,)),
                dma((4,)),
                dma((8,)),
                dma((2,)),
                dma((4 * NZ,)),
                dma((8 * H,)),
                dma((2,)),
                dma((2,)),
                dma((2 * S,)),
                dma((2 * NZ,)),
                dma((2 * S,)),
            ],
            compiler_params=pltpu.CompilerParams(
                collective_id=0, has_side_effects=True, vmem_limit_bytes=60 * 2**20
            ),
        )(modality, gain_text, gain_image, tokens, cotangent, text_weight, image_weight)
        outs = pl.pallas_call(
            functools.partial(finish, dims),
            out_shape=(
                jax.ShapeDtypeStruct((T, E), BF16),
                jax.ShapeDtypeStruct((T, D), BF16),
                jax.ShapeDtypeStruct((WR, WC), F32),
                jax.ShapeDtypeStruct((WR, WC), F32),
                jax.ShapeDtypeStruct((1, D), F32),
                jax.ShapeDtypeStruct((1, D), F32),
            ),
            in_specs=[vmem] * 9,
            out_specs=(vmem,) * 6,
            scratch_shapes=[pltpu.VMEM((T, D), F32)],
            compiler_params=pltpu.CompilerParams(vmem_limit_bytes=24 * 2**20),
        )(modality, gain_text, gain_image, tokens, *parts)
        return (*outs[:4], outs[4].reshape(D), outs[5].reshape(D))

    rows = P(("dp", "text", "image"), None)
    text_at, image_at = P(("dp", "image"), "text"), P(("dp", "text"), "image")
    return jax.shard_map(
        shards,
        mesh=mesh,
        in_specs=(rows, P(("dp", "text", "image")), P(), P(), text_at, image_at, rows),
        out_specs=(rows, rows, text_at, image_at, P(), P()),
        check_vma=False,
    )
```

time: 1350 us -> 139 us (0.10)
  waiting for transfers between devices: 1050 us -> 0 us
  blocking collectives: 201 us -> 0 us
  Pallas kernels: 0 us -> 130 us
  matrix products: 43.5 us -> 0 us
  other arithmetic: 19.9 us -> 0 us
  between operations: 15 us -> 0.72 us
    reduce_scatter x4 -> x0, waiting for transfers between devices: 636 us -> none  [the longest x1 301 us: shards(): lax.psum_scatter(weight_term(text_rows, text_grad_cols), ('dp', 'image'),...]
    all_gather x4 -> x0, waiting for transfers between devices: 404 us -> none  [the longest x1 228 us: shards(): lax.all_gather(text_weight, ('dp', 'image'), axis=0, tiled=True)]
    psum x1 -> x0, blocking collectives: 150 us -> none  [shards(): gain_grads = lax.psum((text_term, image_term), ('dp', 'text', 'image'))]
    pallas_call x0 -> x2, Pallas kernels: none -> 130 us  [the longest x1 126 us: shards(): pl.pallas_call(functools.partial(layer, dims), out_shape=(jax.ShapeDtypeS...]
    all_to_all x2 -> x0, blocking collectives: 51.1 us -> none  [the longest x1 36.7 us: shards(): lax.all_to_all(image_up, 'image', split_axis=1, concat_axis=0, tiled=True)]
    dot_general x6 -> x0, matrix products: 43.5 us -> none  [the longest x2 16.2 us: weight_term(): lax.dot_general(left_rows, upstream, (((0,), (0,)), ((), ())), preferred_...]
  transfers between devices with their start and end apart: 10 -> 0, of which waited for: 9 -> 0; matrix products, arithmetic and copies ran while one was open for 5% -> 0% of each run, Pallas kernels for 0% -> 0%
where the time goes in v2:
time: 139 us; the launch traced here: 136 us
  Pallas kernels  130 us (94%)
  local copies, waits for them, and re-layouts  5.47 us (4%)
    pallas_call x1, Pallas kernels, shards(): pl.pallas_call(functools.partial(layer, dims), out_shape=(jax.ShapeDtypeS...  126 us
    unnamed x18, local copies, waits for them, and re-layouts  5.47 us
    pallas_call x1, Pallas kernels, shards(): pl.pallas_call(functools.partial(finish, dims), out_shape=(jax.ShapeDtype...  3.28 us

profile of v2, /device:TPU:2, one launch (start us, length us, event | category | flops | bytes accessed | tf_op | source)
XLA Modules:
  0.0 135.9 jit_solution(4463902990921195007)
XLA Ops:
  0.6 0.0 copy-start
  0.6 0.0 copy-start.7
  0.7 0.0 copy-start.6
  0.7 0.0 copy-start.8
  0.7 126.5 %shard_map.118 = (bf16[8,80,1024]{2,1,0:T(8,128)(2,1)}, bf16[4,2,80,1024]{3,2,1,0:T(8,128)(2,1)}, f32[2,128,512]{2,1,0:T(8,128)}, bf16[2,128,512]{2,1,0:T(8,128)(2,1)}, f32[8,16,128]{2,1,0:T(8,128)}) custom-call(s32[1,128]{1,0:T(1,128)} %bitcast.9, f32[1,4096]{1,0:T(1,128)} %bitcast.5, f32[1,4096]{1,0:T(1,128)} %bitcast.7, bf16[128,4096]{1,0:T(8,128)(2,1)} %tok_ref.1, ...), custom_call_target="tpu_custom_call" | custom-call | tf_op jit(solution)/shard_map/pallas_call | solution.py:735
  127.1 0.0 copy-done
  127.2 0.0 copy-done.7
  127.2 0.0 copy-done.6
  127.2 0.0 copy-done.8
  127.2 0.0 copy-start.1
  127.2 1.3 copy-done.1
  128.5 0.0 copy-start.2
  128.5 1.3 copy-done.2
  129.8 0.0 copy-start.3
  129.8 1.0 copy-done.3
  130.9 0.0 copy-start.4
  130.9 0.9 copy-done.4
  131.8 0.0 copy-start.5
  131.8 0.8 copy-done.5
  132.7 3.3 %shard_map.119 = (bf16[128,4096]{1,0:T(8,128)(2,1)}, bf16[128,4096]{1,0:T(8,128)(2,1)}, f32[128,512]{1,0:T(8,128)}, f32[128,512]{1,0:T(8,128)}, f32[1,4096]{1,0:T(1,128)}, /*index=5*/f32[1,4096]{1,0:T(1,128)}) custom-call(s32[1,128]{1,0:T(1,128)S(1)} %bitcast.10, f32[1,4096]{1,0:T(1,128)S(1)} %bitcast.6, f32[1,4096]{1,0:T(1,128)S(1)} %bitcast.8, ...), custom_call_target="tpu_custom_call" | custom-call | tf_op jit(solution)/shard_map/pallas_call | solution.py:803
Async XLA Ops:
  0.6 126.5 %copy-start = (bf16[128,4096]{1,0:T(8,128)(2,1)S(1)}, bf16[128,4096]{1,0:T(8,128)(2,1)}, u32[]{:S(2)}) copy-start(bf16[128,4096]{1,0:T(8,128)(2,1)} %tok_ref.1) | copy-start | bytes 3145732
  0.6 126.5 %copy-start.7 = (f32[4096]{0:T(1024)S(1)}, f32[4096]{0:T(1024)}, u32[]{:S(2)}) copy-start(f32[4096]{0:T(1024)} %param.10) | copy-start | bytes 49156
  0.7 126.5 %copy-start.6 = (f32[4096]{0:T(1024)S(1)}, f32[4096]{0:T(1024)}, u32[]{:S(2)}) copy-start(f32[4096]{0:T(1024)} %param.9) | copy-start | bytes 49156
  0.7 126.5 %copy-start.8 = (s32[128]{0:T(128)S(1)}, s32[128]{0:T(128)}, u32[]{:S(2)}) copy-start(s32[128]{0:T(128)} %param.8) | copy-start | bytes 1540
  127.2 1.3 copy-start.1
  128.5 1.3 copy-start.2
  129.8 1.0 copy-start.3
  130.9 0.9 copy-start.4
  131.8 0.8 copy-start.5

commit v3 on v2

--- a/solution.py
+++ b/solution.py
@@ -41,11 +41,11 @@
 def layer(
     dims,
     mod_ref, gt_ref, gi_ref, tok_in, cot_in, wt_in, wi_in,
-    qf_out, df_out, dw_out, dwx_out, gain_out,
-    tok_ref, cot_ref, pick, flag, inv, work, gacc,
+    q_out, tg_out, dwt_out, dwi_out, ggt_out, ggi_out,
+    tok_ref, cot_ref, pick, place, flag, inv, work, grads, gacc,
     xs, gs, xall, gall, w, qp, dp, qr, dm, dr, qf, df,
     dw_own, dw_peer, dw_sum, ring, dw_x, dw_xr, dw_end,
-    g_core, g_b, g_z, g_c,
+    g_core, g_b, g_z, g_c, gain_ref,
     local, send, x1, x2, g1, g2, wx, w1, w2, q1, q2, d0, d1, d2, e1, e2, e3, s1, s2, s3, s4,
 ):
     S, ZL, T, R, DS, ES = dims
@@ -113,12 +113,17 @@
 
     pl.semaphore_signal(barrier, inc=1, device_id=partner, device_id_type=MESH)
 
-    flag_row, flag_col, rank_row, _ = ranks(mod_ref[...], T)
+    flag_row, flag_col, rank_row, rank_col = ranks(mod_ref[...], T)
     flag[...] = flag_col
     slot = lax.broadcasted_iota(jnp.int32, (R, T), 0).astype(F32)
     spot = lax.broadcasted_iota(jnp.int32, (R, T), 1).astype(F32)
     pick[:R] = jnp.where((rank_row == slot) & (flag_row > 0.5), 1.0, 0.0).astype(BF16)
     pick[R:] = jnp.where((spot - rank_row == slot) & (flag_row < 0.5), 1.0, 0.0).astype(BF16)
+
+    slot = lax.broadcasted_iota(jnp.int32, (T, R), 1).astype(F32)
+    spot = lax.broadcasted_iota(jnp.int32, (T, R), 0).astype(F32)
+    place[0] = jnp.where((rank_col == slot) & (flag_col > 0.5), 1.0, 0.0).astype(BF16)
+    place[1] = jnp.where((spot - rank_col == slot) & (flag_col < 0.5), 1.0, 0.0).astype(BF16)
 
     def w_at(m, g, from_z, from_core, part=None):
         from_zh, from_zl = lax.div(from_z, ZL), lax.rem(from_z, ZL)
@@ -209,18 +214,19 @@
         squares = squares + part * part
     inv[...] = lax.rsqrt(jnp.sum(squares, axis=1, keepdims=True) / D + EPSILON)
 
-    @pl.loop(0, S * ZL)
-    def _(i):
-        c, zq = lax.div(i, ZL), lax.rem(i, ZL)
-        at = pl.ds(pl.multiple_of(zq * (S * CH) + c * CH, CH), CH)
-        to = pl.ds(pl.multiple_of(zq * CH, CH), CH)
-        unit = tok_ref[:, at].astype(F32) * inv[...]
-        gains = jnp.where(flag[...] > 0.5, gt_ref[:, at], gi_ref[:, at])
-        normed = (unit * gains).astype(BF16)
+    scale = jnp.broadcast_to(inv[...], (T, CH))
+    is_text = jnp.broadcast_to(flag[...], (T, CH)) > 0.5
+
+    @pl.loop(0, S)
+    def _(c):
         half, g = lax.rem(c, 2), lax.div(c, 2)
-        chosen = dot_nn(pick[...], normed).astype(BF16)
-        xs[half, g, :, to] = chosen[:R]
-        xs[2 + half, g, :, to] = chosen[R:]
+        for zq in range(ZL):
+            at = pl.ds(pl.multiple_of(zq * (S * CH) + c * CH, CH), CH)
+            gains = jnp.where(is_text, gt_ref[:, at], gi_ref[:, at])
+            normed = (tok_ref[:, at].astype(F32) * scale * gains).astype(BF16)
+            chosen = dot_nn(pick[...], normed).astype(BF16)
+            xs[half, g, :, zq * CH:(zq + 1) * CH] = chosen[:R]
+            xs[2 + half, g, :, zq * CH:(zq + 1) * CH] = chosen[R:]
 
     def spread(m, kind):
         block = xall.at[token_rows(m, bc(m), odd(m) + kind - 2 * odd(m) * kind)]
@@ -278,24 +284,30 @@
             if t < H:
                 ring_w(t + 1, m, g)
 
-    @pl.loop(0, 2)
-    def _(m):
-        arrived(xall.at[token_rows(m, bc(m), 1 - odd(m))], x1.at[m])
-        spread(m, 1)
-
+    ring_w_on(1, 0)
     pass_on_grads(1)
-    ring_w_on(1, 0)
     pass_on_grads(3)
     pass_on_grads(2)
     ring_w_on(1, 1)
+
+    @pl.loop(0, 2)
+    def _(m):
+        arrived(xall.at[token_rows(m, bc(m), 1 - odd(m))], x1.at[m])
+        spread(m, 1)
+
+    if H > 1:
+        ring_w_on(2, 0)
     both(spread_on, 0)
     if H > 1:
-        ring_w_on(2, 0)
         ring_w_on(2, 1)
+    for t in range(3, H):
+        ring_w_on(t, 0)
     both(spread_on, 1)
-    for t in range(3, H + 1):
-        ring_w_on(t, 0)
+    for t in range(3, H):
         ring_w_on(t, 1)
+    if H > 2:
+        ring_w_on(H, 0)
+        ring_w_on(H, 1)
     both(spread_end, 0)
     both(spread_end, 1)
 
@@ -306,27 +318,38 @@
             b = lax.rem(bc(m) + S - j, S)
             arrived(gall.at[token_rows(m, b, 1 - odd(m))], g2.at[m * S + j])
 
-    def weight_grad(lane):
-        m, g = lane // 2, lane % 2
-
-        @pl.loop(0, ZL)
-        def _(zq):
+    def lane_of(i):
+        m = i % 2 if isinstance(i, int) else lax.rem(i, 2)
+        far = 1 - (i // 2 if isinstance(i, int) else lax.div(i, 2))
+        g = group(m) + (1 - 2 * group(m)) * far
+        return m, g, m * 2 + g
+
+    def weight_grad(m, first_offset, tiles):
+        @pl.loop(0, tiles)
+        def _(n):
+            zq = lax.rem(zl + first_offset + n * (ZL - 2), ZL)
             at = pl.ds(pl.multiple_of(zq * CH, CH), CH)
-            left = xall[pl.ds(m * 2 * S, 2 * S), g, :, at].reshape(2 * S * R, CH)
+            left = jnp.concatenate(
+                [xall[pl.ds(m * 2 * S, 2 * S), g, :, at].reshape(2 * S * R, CH) for g in range(2)], axis=1
+            )
             for half in range(2):
                 right = gall[pl.ds(m * 2 * S, 2 * S), :, half * WC:(half + 1) * WC]
                 work[:, half * WC:(half + 1) * WC] = dot_tn(left, right.reshape(2 * S * R, WC))
-            upper, lower = work[:WR, :WC], work[WR:, WC:]
-            cross = (work[:WR, WC:], work[WR:, :WC])
-            first, second = cross[m], cross[1 - m]
             low = core == 0
-            dw_own[lane * NZ + zq] = jnp.where(low, upper, first).astype(BF16)
-            dw_own[lane * NZ + ZL + zq] = jnp.where(low, second, lower).astype(BF16)
-            dw_peer[lane * NZ + zq] = jnp.where(low, first, upper).astype(BF16)
-            dw_peer[lane * NZ + ZL + zq] = jnp.where(low, lower, second).astype(BF16)
-            for part in range(2):
-                to = lane * NZ + part * ZL + zq
-                push(dw_peer.at[to], dw_sum.at[to], send.at[10], e1.at[to], partner).start()
+            for g in range(2):
+                top, mid, end = g * CH, g * CH + WR, (g + 1) * CH
+                base = (m * 2 + g) * NZ + zq
+                upper, lower = work[top:mid, :WC], work[mid:end, WC:]
+                cross = (work[top:mid, WC:], work[mid:end, :WC])
+                first = jnp.where(m == 0, cross[0], cross[1])
+                second = jnp.where(m == 0, cross[1], cross[0])
+                dw_own[base] = jnp.where(low, upper, first).astype(BF16)
+                dw_own[base + ZL] = jnp.where(low, second, lower).astype(BF16)
+                dw_peer[base] = jnp.where(low, first, upper).astype(BF16)
+                dw_peer[base + ZL] = jnp.where(low, lower, second).astype(BF16)
+                for part in range(2):
+                    to = base + part * ZL
+                    push(dw_peer.at[to], dw_sum.at[to], send.at[10], e1.at[to], partner).start()
 
     def share(lane, to):
         return dw_own[lane * NZ + to].astype(F32) + dw_sum[lane * NZ + to].astype(F32)
@@ -537,10 +560,10 @@
     def steps(t, *lanes):
         if t < H:
             for lane in lanes:
-                ring_step(t, lane)
+                ring_step(t, lane_of(lane)[2])
 
     gacc[...] = jnp.zeros_like(gacc)
-    weight_grad(0)
+    both(weight_grad, 0, 1)
 
     @pl.loop(0, 4 * NZ)
     def _(i):
@@ -548,38 +571,38 @@
         m, g = lax.div(lane, 2), lax.rem(lane, 2)
         arrived(w_at(m, g, k, 1 - core), w2.at[lane * NZ + k])
 
-    both(input_grads_first)
-    ring_start(0)
-    weight_grad(1)
-    ring_start(1)
-    steps(1, 0)
-    both(input_grads_last)
+    input_grads_first(0)
+    ring_start(lane_of(0)[2])
+    ring_start(lane_of(1)[2])
+    input_grads_first(1)
+    ring_start(lane_of(2)[2])
+    ring_start(lane_of(3)[2])
+    @pl.loop(0, 2)
+    def _(m):
+        weight_grad(m, 1, 2)
+        ring_step(1, lane_of(m)[2])
+        ring_step(1, lane_of(m + 2)[2])
+
+    input_grads_last(0)
+    input_grads_last(1)
     gains_core()
     input_grads_mid(0)
-    weight_grad(2)
-    ring_start(2)
-    steps(1, 1)
     input_grads_mid(1)
-    weight_grad(3)
-    ring_start(3)
-    steps(1, 2)
-    steps(2, 0)
+
+    both(weight_grad, 2, 1)
+
+    gains_b()
+    steps(2, 0, 1)
     queries(0)
-    steps(1, 3)
-    steps(2, 1)
+    steps(2, 2, 3)
     queries(1)
-    gains_b()
-    steps(2, 2, 3)
+    steps(3, 0, 1)
+    gains_z()
+    both(grad_sums)
+    steps(3, 2, 3)
     query_sums(0)
-    steps(3, 0)
+    gains_c()
     query_sums(1)
-    steps(3, 1)
-    gains_z()
-    grad_sums(0)
-    steps(3, 2)
-    grad_sums(1)
-    steps(3, 3)
-    gains_c()
 
     @pl.loop(0, 2)
     def _(m):
@@ -593,12 +616,18 @@
         def _(j):
             arrived(qf.at[m * S + lax.rem(bc(m) + S - j, S)], q2.at[m * S + j])
 
+    @pl.loop(0, S)
+    def _(b):
+        full = dot_nn(place[0], qf[b]) + dot_nn(place[1], qf[S + b])
+        cot_ref[:, pl.ds(pl.multiple_of(b * ES, ES), ES)] = full.astype(BF16)
+
     stores = [
-        pltpu.make_async_copy(qf, qf_out, local.at[0]),
-        pltpu.make_async_copy(df, df_out, local.at[1]),
-        pltpu.make_async_copy(dw_end, dw_out, local.at[2]),
-        pltpu.make_async_copy(dw_xr, dwx_out, local.at[3]),
-        pltpu.make_async_copy(g_c, gain_out, local.at[4]),
+        pltpu.make_async_copy(cot_ref, q_out, local.at[0]),
+        pltpu.make_async_copy(tok_ref, tg_out, local.at[1]),
+        pltpu.make_async_copy(dw_end.at[0], dwt_out, local.at[2]),
+        pltpu.make_async_copy(dw_end.at[1], dwi_out, local.at[3]),
+        pltpu.make_async_copy(gain_ref.at[0], ggt_out, local.at[4]),
+        pltpu.make_async_copy(gain_ref.at[1], ggi_out, local.at[5]),
     ]
     stores[0].start()
 
@@ -606,13 +635,23 @@
     def _(m):
         arrived(df.at[m * 2 + 1 - odd(m)], d2.at[m])
 
+    products = jnp.zeros((T, CH), F32)
+    for c in range(S):
+        half, g = c % 2, c // 2
+        normed_grad = dot_nn(place[0], df[half, g]) + dot_nn(place[1], df[2 + half, g])
+        for zq in range(ZL):
+            at = slice(zq * S * CH + c * CH, zq * S * CH + (c + 1) * CH)
+            gains = jnp.where(flag[...] > 0.5, gt_ref[:, at], gi_ref[:, at])
+            part = normed_grad[:, zq * CH:(zq + 1) * CH] * gains
+            grads[:, at] = part
+            products = products + part * tok_ref[:, at].astype(F32)
+    scale = inv[...]
+    along = jnp.sum(products, axis=1, keepdims=True) / D * scale * scale
+    for i in range(S * ZL):
+        at = slice(i * CH, (i + 1) * CH)
+        tok_ref[:, at] = (scale * (grads[:, at] - tok_ref[:, at].astype(F32) * along)).astype(BF16)
+
     stores[1].start()
-
-    @pl.loop(0, 2)
-    def _(m):
-        dw_end[m] = ring_end(m * 2 + group(m))
-
-    stores[2].start()
 
     @pl.loop(0, 2)
     def _(m):
@@ -620,12 +659,28 @@
         def _(k):
             arrived(g_c.at[m * S + lax.rem(cc(m) + S - k, S)], s4.at[m * S + k])
 
+    for m, gain in ((0, gt_ref), (1, gi_ref)):
+        for half in range(2):
+            total = g_c[m * S + half]
+            for k in range(half + 2, S, 2):
+                total = total + g_c[m * S + k]
+            for g in range(S // 2):
+                for i in range(GR):
+                    zq, off = (i * 128) // CH, (i * 128) % CH
+                    first = zq * S * CH + (half + 2 * g) * CH + off
+                    at = slice(first, first + 128)
+                    gain_ref[m, :, at] = total[g * GR + i:g * GR + i + 1, :] / gain[:, at]
+
     stores[4].start()
-
-    @pl.loop(0, 2)
-    def _(m):
+    stores[5].start()
+
+    @pl.loop(0, 2)
+    def _(m):
+        own = ring_end(m * 2 + group(m))
         arrived(dw_xr.at[m], e3.at[m])
-
+        dw_end[m] = own + dw_xr[m].astype(F32)
+
+    stores[2].start()
     stores[3].start()
 
     sent(w.at[pl.ds(0, 4)], send.at[1])
@@ -656,60 +711,19 @@
         store.wait()
 
 
-def finish(
-    dims,
-    mod_ref, gt_ref, gi_ref, tok_ref, qf, df, dw_ref, dwx_ref, gain_ref,
-    q_out, tg_out, dwt_out, dwi_out, ggt_out, ggi_out,
-    grads,
-):
-    S, ZL, T, R, DS, ES = dims
-    CH = DS // ZL
-    GR = DS // 128
-    D = DS * S
-    _, flag, _, rank_col = ranks(mod_ref[...], T)
-    slot = lax.broadcasted_iota(jnp.int32, (T, R), 1).astype(F32)
-    spot = lax.broadcasted_iota(jnp.int32, (T, R), 0).astype(F32)
-    text = jnp.where((rank_col == slot) & (flag > 0.5), 1.0, 0.0).astype(BF16)
-    image = jnp.where((spot - rank_col == slot) & (flag < 0.5), 1.0, 0.0).astype(BF16)
-
-    squares = jnp.zeros((T, CH), F32)
-    products = jnp.zeros((T, CH), F32)
-    for c in range(S):
-        half, g = c % 2, c // 2
-        normed_grad = dot_nn(text, df[half, g]) + dot_nn(image, df[2 + half, g])
-        for zq in range(ZL):
-            at = slice(zq * S * CH + c * CH, zq * S * CH + (c + 1) * CH)
-            gains = jnp.where(flag > 0.5, gt_ref[:, at], gi_ref[:, at])
-            part = normed_grad[:, zq * CH:(zq + 1) * CH] * gains
-            token = tok_ref[:, at].astype(F32)
-            grads[:, at] = part
-            squares = squares + token * token
-            products = products + part * token
-    inv = lax.rsqrt(jnp.sum(squares, axis=1, keepdims=True) / D + EPSILON)
-    along = jnp.sum(products, axis=1, keepdims=True) / D * inv * inv
-
-    for i in range(S * ZL):
-        at = slice(i * CH, (i + 1) * CH)
-        tg_out[:, at] = (inv * (grads[:, at] - tok_ref[:, at].astype(F32) * along)).astype(BF16)
-
-    for b in range(S):
-        full = dot_nn(text, qf[b]) + dot_nn(image, qf[S + b])
-        q_out[:, b * ES:(b + 1) * ES] = full.astype(BF16)
-
-    dwt_out[...] = dw_ref[0] + dwx_ref[0].astype(F32)
-    dwi_out[...] = dw_ref[1] + dwx_ref[1].astype(F32)
-
-    for m, out, gain in ((0, ggt_out, gt_ref), (1, ggi_out, gi_ref)):
-        for half in range(2):
-            total = gain_ref[m * S + half]
-            for k in range(half + 2, S, 2):
-                total = total + gain_ref[m * S + k]
-            for g in range(S // 2):
-                for i in range(GR):
-                    zq, off = (i * 128) // CH, (i * 128) % CH
-                    first = zq * S * CH + (half + 2 * g) * CH + off
-                    at = slice(first, first + 128)
-                    out[:, at] = total[g * GR + i:g * GR + i + 1, :] / gain[:, at]
+def hand_on(*refs):
+    came, gone = refs[-2:]
+    count = (len(refs) - 2) // 3
+    sources, targets, held = refs[:count], refs[count:2 * count], refs[2 * count:3 * count]
+    loads = [pltpu.make_async_copy(sources[i], held[i], came.at[i]) for i in range(count)]
+    stores = [pltpu.make_async_copy(held[i], targets[i], gone.at[i]) for i in range(count)]
+    for load in loads:
+        load.start()
+    for load, store in zip(loads, stores):
+        load.wait()
+        store.start()
+    for store in stores:
+        store.wait()
 
 
 def solution(mesh):
@@ -732,24 +746,28 @@
         modality, gain_text, gain_image = (
             modality.reshape(1, T), gain_text.reshape(1, D), gain_image.reshape(1, D)
         )
+        shapes = (
+            jax.ShapeDtypeStruct((T, E), BF16),
+            jax.ShapeDtypeStruct((T, D), BF16),
+            jax.ShapeDtypeStruct((WR, WC), F32),
+            jax.ShapeDtypeStruct((WR, WC), F32),
+            jax.ShapeDtypeStruct((1, D), F32),
+            jax.ShapeDtypeStruct((1, D), F32),
+        )
         parts = pl.pallas_call(
             functools.partial(layer, dims),
-            out_shape=(
-                jax.ShapeDtypeStruct((2 * S, R, ES), BF16),
-                jax.ShapeDtypeStruct((4, 2, R, DS), BF16),
-                jax.ShapeDtypeStruct((2, WR, WC), F32),
-                jax.ShapeDtypeStruct((2, WR, WC), BF16),
-                jax.ShapeDtypeStruct((2 * S, 2 * GR, 128), F32),
-            ),
+            out_shape=shapes,
             in_specs=[vmem] * 3 + [anywhere] * 4,
-            out_specs=(anywhere,) * 5,
+            out_specs=(anywhere,) * 6,
             scratch_shapes=[
                 pltpu.VMEM((T, D), BF16),
                 pltpu.VMEM((T, E), BF16),
                 pltpu.VMEM((2 * R, T), BF16),
+                pltpu.VMEM((2, T, R), BF16),
                 pltpu.VMEM((T, 1), F32),
                 pltpu.VMEM((T, 1), F32),
-                pltpu.VMEM((CH, ES), F32),
+                pltpu.VMEM((2 * CH, ES), F32),
+                pltpu.VMEM((T, D), F32),
                 pltpu.VMEM((4, 1, DS), F32),
                 pltpu.VMEM((4, 2, R, DS), BF16),
                 pltpu.VMEM((2 * S, R, ES), BF16),
@@ -774,7 +792,8 @@
                 pltpu.VMEM((2 * S, 2 * GR, 128), F32),
                 pltpu.VMEM((2 * NZ, 2 * GR, 128), F32),
                 pltpu.VMEM((2 * S, 2 * GR, 128), F32),
-                dma((5,)),
+                pltpu.VMEM((2, 1, D), F32),
+                dma((6,)),
                 dma((23,)),
                 dma((2,)),
                 dma((16,)),
@@ -801,20 +820,13 @@
             ),
         )(modality, gain_text, gain_image, tokens, cotangent, text_weight, image_weight)
         outs = pl.pallas_call(
-            functools.partial(finish, dims),
-            out_shape=(
-                jax.ShapeDtypeStruct((T, E), BF16),
-                jax.ShapeDtypeStruct((T, D), BF16),
-                jax.ShapeDtypeStruct((WR, WC), F32),
-                jax.ShapeDtypeStruct((WR, WC), F32),
-                jax.ShapeDtypeStruct((1, D), F32),
-                jax.ShapeDtypeStruct((1, D), F32),
-            ),
-            in_specs=[vmem] * 9,
-            out_specs=(vmem,) * 6,
-            scratch_shapes=[pltpu.VMEM((T, D), F32)],
-            compiler_params=pltpu.CompilerParams(vmem_limit_bytes=24 * 2**20),
-        )(modality, gain_text, gain_image, tokens, *parts)
+            hand_on,
+            out_shape=shapes,
+            in_specs=[anywhere] * 6,
+            out_specs=(anywhere,) * 6,
+            scratch_shapes=[pltpu.VMEM(a.shape, a.dtype) for a in shapes] + [dma((6,)), dma((6,))],
+            compiler_params=pltpu.CompilerParams(vmem_limit_bytes=60 * 2**20),
+        )(*parts)
         return (*outs[:4], outs[4].reshape(D), outs[5].reshape(D))
 
     rows = P(("dp", "text", "image"), None)

time: 139 us -> 119 us (0.86); the launches traced: 136 us -> 118 us
  Pallas kernels: 130 us -> 117 us
  local copies, waits for them, and re-layouts: 5.47 us -> 0 us
    pallas_call x2, Pallas kernels: 130 us -> 117 us  [the longest x1 114 us: shards(): pl.pallas_call(functools.partial(layer, dims), out_shape=shapes, in_specs...]
    unnamed x18 -> x0, local copies, waits for them, and re-layouts: 5.47 us -> none
where the time goes in v3:
time: 119 us; the launch traced here: 118 us
  Pallas kernels  117 us (98%)
    pallas_call x1, Pallas kernels, shards(): pl.pallas_call(functools.partial(layer, dims), out_shape=shapes, in_specs...  114 us
    pallas_call x1, Pallas kernels, shards(): pl.pallas_call(hand_on, out_shape=shapes, in_specs=[anywhere] * 6, out_sp...  2.81 us

profile of v3, /device:TPU:2, one launch (start us, length us, event | category | flops | bytes accessed | tf_op | source)
XLA Modules:
  0.0 117.8 jit_solution(17048859575847815490)
XLA Ops:
  0.6 114.2 %shard_map.118 = (bf16[128,4096]{1,0:T(8,128)(2,1)}, bf16[128,4096]{1,0:T(8,128)(2,1)}, f32[128,512]{1,0:T(8,128)}, f32[128,512]{1,0:T(8,128)}, f32[1,4096]{1,0:T(1,128)}, /*index=5*/f32[1,4096]{1,0:T(1,128)}) custom-call(s32[1,128]{1,0:T(1,128)} %bitcast.7, f32[1,4096]{1,0:T(1,128)} %bitcast.5, f32[1,4096]{1,0:T(1,128)} %bitcast.6, ...), custom_call_target="tpu_custom_call" | custom-call | tf_op jit(solution)/shard_map/pallas_call | solution.py:757
  114.8 2.8 %shard_map.119 = (bf16[128,4096]{1,0:T(8,128)(2,1)}, bf16[128,4096]{1,0:T(8,128)(2,1)}, f32[128,512]{1,0:T(8,128)}, f32[128,512]{1,0:T(8,128)}, f32[1,4096]{1,0:T(1,128)}, /*index=5*/f32[1,4096]{1,0:T(1,128)}) custom-call(bf16[128,4096]{1,0:T(8,128)(2,1)} %get-tuple-element.18.refs_0_, bf16[128,4096]{1,0:T(8,128)(2,1)} %get-tuple-element.19.refs_1_, ...), custom_call_target="tpu_custom_call" | custom-call | tf_op jit(solution)/shard_map/pallas_call | solution.py:822

commit v4 on v3

--- a/solution.py
+++ b/solution.py
@@ -113,18 +113,6 @@
 
     pl.semaphore_signal(barrier, inc=1, device_id=partner, device_id_type=MESH)
 
-    flag_row, flag_col, rank_row, rank_col = ranks(mod_ref[...], T)
-    flag[...] = flag_col
-    slot = lax.broadcasted_iota(jnp.int32, (R, T), 0).astype(F32)
-    spot = lax.broadcasted_iota(jnp.int32, (R, T), 1).astype(F32)
-    pick[:R] = jnp.where((rank_row == slot) & (flag_row > 0.5), 1.0, 0.0).astype(BF16)
-    pick[R:] = jnp.where((spot - rank_row == slot) & (flag_row < 0.5), 1.0, 0.0).astype(BF16)
-
-    slot = lax.broadcasted_iota(jnp.int32, (T, R), 1).astype(F32)
-    spot = lax.broadcasted_iota(jnp.int32, (T, R), 0).astype(F32)
-    place[0] = jnp.where((rank_col == slot) & (flag_col > 0.5), 1.0, 0.0).astype(BF16)
-    place[1] = jnp.where((spot - rank_col == slot) & (flag_col < 0.5), 1.0, 0.0).astype(BF16)
-
     def w_at(m, g, from_z, from_core, part=None):
         from_zh, from_zl = lax.div(from_z, ZL), lax.rem(from_z, ZL)
         half = from_core + (from_zh - from_core) * m
@@ -172,16 +160,26 @@
             block = w_at(m, g, lax.rem(z + H, NZ), core)
             push(block, block, send.at[1], w2.at[lane * NZ + lax.rem(z + H, NZ)], partner).start()
 
-    loads[0].wait()
-    loads[1].wait()
     pl.semaphore_wait(barrier, 2 * (S - 1) + NZ)
-
-    @pl.loop(0, 2)
-    def _(m):
-        mine = w_at(m, group(m), z, core)
-        push(mine, mine, send.at[17], wx.at[m], twin(m)).start()
-        ring_w(1, m, group(m))
-        push(mine, mine, send.at[1], w2.at[(m * 2 + group(m)) * NZ + z], partner).start()
+    for m, mine in ((0, wt_in), (1, wi_in)):
+        lane = m * 2 + group(m)
+        place_at = w_at(m, group(m), z, core)
+        for way, step in ((0, 1), (1, NZ - 1)):
+            push(mine, place_at, send.at[18], w1.at[way * H * 4 + lane], along_z(step)).start()
+        push(mine, place_at, send.at[17], wx.at[m], twin(m)).start()
+        push(mine, place_at, send.at[1], w2.at[lane * NZ + z], partner).start()
+
+    flag_row, flag_col, rank_row, rank_col = ranks(mod_ref[...], T)
+    flag[...] = flag_col
+    slot = lax.broadcasted_iota(jnp.int32, (R, T), 0).astype(F32)
+    spot = lax.broadcasted_iota(jnp.int32, (R, T), 1).astype(F32)
+    pick[:R] = jnp.where((rank_row == slot) & (flag_row > 0.5), 1.0, 0.0).astype(BF16)
+    pick[R:] = jnp.where((spot - rank_row == slot) & (flag_row < 0.5), 1.0, 0.0).astype(BF16)
+
+    slot = lax.broadcasted_iota(jnp.int32, (T, R), 1).astype(F32)
+    spot = lax.broadcasted_iota(jnp.int32, (T, R), 0).astype(F32)
+    place[0] = jnp.where((rank_col == slot) & (flag_col > 0.5), 1.0, 0.0).astype(BF16)
+    place[1] = jnp.where((spot - rank_col == slot) & (flag_col < 0.5), 1.0, 0.0).astype(BF16)
 
     loads[2].wait()
 
@@ -284,6 +282,8 @@
             if t < H:
                 ring_w(t + 1, m, g)
 
+    loads[0].wait()
+    loads[1].wait()
     ring_w_on(1, 0)
     pass_on_grads(1)
     pass_on_grads(3)
@@ -305,22 +305,17 @@
     both(spread_on, 1)
     for t in range(3, H):
         ring_w_on(t, 1)
-    if H > 2:
-        ring_w_on(H, 0)
-        ring_w_on(H, 1)
-    both(spread_end, 0)
-    both(spread_end, 1)
-
-    @pl.loop(0, 2)
-    def _(m):
+    def rows_complete(m):
+        spread_end(m, 0)
+        spread_end(m, 1)
+
         @pl.loop(0, S)
         def _(j):
             b = lax.rem(bc(m) + S - j, S)
             arrived(gall.at[token_rows(m, b, 1 - odd(m))], g2.at[m * S + j])
 
     def lane_of(i):
-        m = i % 2 if isinstance(i, int) else lax.rem(i, 2)
-        far = 1 - (i // 2 if isinstance(i, int) else lax.div(i, 2))
+        m, far = lax.div(jnp.int32(i), 2), 1 - lax.rem(jnp.int32(i), 2)
         g = group(m) + (1 - 2 * group(m)) * far
         return m, g, m * 2 + g
 
@@ -563,7 +558,17 @@
                 ring_step(t, lane_of(lane)[2])
 
     gacc[...] = jnp.zeros_like(gacc)
-    both(weight_grad, 0, 1)
+    def ring_starts(m):
+        ring_start(lane_of(2 * m)[2])
+        ring_start(lane_of(2 * m + 1)[2])
+
+    rows_complete(0)
+    weight_grad(0, 0, 1)
+    ring_w_on(H, 0)
+    ring_w_on(H, 1)
+    rows_complete(1)
+    weight_grad(1, 0, 1)
+    ring_starts(0)
 
     @pl.loop(0, 4 * NZ)
     def _(i):
@@ -572,54 +577,37 @@
         arrived(w_at(m, g, k, 1 - core), w2.at[lane * NZ + k])
 
     input_grads_first(0)
-    ring_start(lane_of(0)[2])
-    ring_start(lane_of(1)[2])
+    ring_starts(1)
     input_grads_first(1)
-    ring_start(lane_of(2)[2])
-    ring_start(lane_of(3)[2])
+
     @pl.loop(0, 2)
     def _(m):
         weight_grad(m, 1, 2)
-        ring_step(1, lane_of(m)[2])
-        ring_step(1, lane_of(m + 2)[2])
-
-    input_grads_last(0)
-    input_grads_last(1)
+        ring_step(1, lane_of(2 * m)[2])
+        ring_step(1, lane_of(2 * m + 1)[2])
+
+    both(input_grads_last)
     gains_core()
-    input_grads_mid(0)
-    input_grads_mid(1)
-
     both(weight_grad, 2, 1)
-
+    steps(2, 0, 1)
+    both(input_grads_mid)
     gains_b()
-    steps(2, 0, 1)
     queries(0)
     steps(2, 2, 3)
     queries(1)
     steps(3, 0, 1)
+    steps(3, 2, 3)
     gains_z()
     both(grad_sums)
-    steps(3, 2, 3)
     query_sums(0)
+    query_sums(1)
     gains_c()
-    query_sums(1)
 
     @pl.loop(0, 2)
     def _(m):
         other = 1 - group(m)
         dw_x[m] = ring_end(m * 2 + other).astype(BF16)
         push(dw_x.at[m], dw_xr.at[m], send.at[20], e3.at[m], twin(m)).start()
-
-    @pl.loop(0, 2)
-    def _(m):
-        @pl.loop(1, S)
-        def _(j):
-            arrived(qf.at[m * S + lax.rem(bc(m) + S - j, S)], q2.at[m * S + j])
-
-    @pl.loop(0, S)
-    def _(b):
-        full = dot_nn(place[0], qf[b]) + dot_nn(place[1], qf[S + b])
-        cot_ref[:, pl.ds(pl.multiple_of(b * ES, ES), ES)] = full.astype(BF16)
 
     stores = [
         pltpu.make_async_copy(cot_ref, q_out, local.at[0]),
@@ -629,8 +617,6 @@
         pltpu.make_async_copy(gain_ref.at[0], ggt_out, local.at[4]),
         pltpu.make_async_copy(gain_ref.at[1], ggi_out, local.at[5]),
     ]
-    stores[0].start()
-
     @pl.loop(0, 2)
     def _(m):
         arrived(df.at[m * 2 + 1 - odd(m)], d2.at[m])
@@ -652,6 +638,19 @@
         tok_ref[:, at] = (scale * (grads[:, at] - tok_ref[:, at].astype(F32) * along)).astype(BF16)
 
     stores[1].start()
+
+    @pl.loop(0, 2)
+    def _(m):
+        @pl.loop(1, S)
+        def _(j):
+            arrived(qf.at[m * S + lax.rem(bc(m) + S - j, S)], q2.at[m * S + j])
+
+    @pl.loop(0, S)
+    def _(b):
+        full = dot_nn(place[0], qf[b]) + dot_nn(place[1], qf[S + b])
+        cot_ref[:, pl.ds(pl.multiple_of(b * ES, ES), ES)] = full.astype(BF16)
+
+    stores[0].start()
 
     @pl.loop(0, 2)
     def _(m):
@@ -714,9 +713,15 @@
 def hand_on(*refs):
     came, gone = refs[-2:]
     count = (len(refs) - 2) // 3
-    sources, targets, held = refs[:count], refs[count:2 * count], refs[2 * count:3 * count]
-    loads = [pltpu.make_async_copy(sources[i], held[i], came.at[i]) for i in range(count)]
-    stores = [pltpu.make_async_copy(held[i], targets[i], gone.at[i]) for i in range(count)]
+    loads, stores = [], []
+    for i in range(count):
+        rows = refs[i].shape[0]
+        step = max(rows // 4, 1)
+        for first in range(0, rows, step):
+            at, sem = pl.ds(first, step), len(loads)
+            held = refs[2 * count + i].at[at]
+            loads.append(pltpu.make_async_copy(refs[i].at[at], held, came.at[sem]))
+            stores.append(pltpu.make_async_copy(held, refs[count + i].at[at], gone.at[sem]))
     for load in loads:
         load.start()
     for load, store in zip(loads, stores):
@@ -824,7 +829,7 @@
             out_shape=shapes,
             in_specs=[anywhere] * 6,
             out_specs=(anywhere,) * 6,
-            scratch_shapes=[pltpu.VMEM(a.shape, a.dtype) for a in shapes] + [dma((6,)), dma((6,))],
+            scratch_shapes=[pltpu.VMEM(a.shape, a.dtype) for a in shapes] + [dma((18,)), dma((18,))],
             compiler_params=pltpu.CompilerParams(vmem_limit_bytes=60 * 2**20),
         )(*parts)
         return (*outs[:4], outs[4].reshape(D), outs[5].reshape(D))

time: 119 us -> 116 us (0.975)
  Pallas kernels: 117 us -> 115 us
    pallas_call x1, Pallas kernels: 114 us -> 112 us  [shards(): pl.pallas_call(functools.partial(layer, dims), out_shape=shapes, in_specs...]
where the time goes in v4:
time: 116 us
  Pallas kernels  115 us (99%)
    pallas_call x1, Pallas kernels, shards(): pl.pallas_call(functools.partial(layer, dims), out_shape=shapes, in_specs...  112 us
    pallas_call x1, Pallas kernels, shards(): pl.pallas_call(hand_on, out_shape=shapes, in_specs=[anywhere] * 6, out_sp...  2.74 us

profile of v4, /device:TPU:2, one launch (start us, length us, event | category | flops | bytes accessed | tf_op | source)
XLA Modules:
  0.0 116.0 jit_solution(16686674898324755109)
XLA Ops:
  0.6 112.4 %shard_map.118 = (bf16[128,4096]{1,0:T(8,128)(2,1)}, bf16[128,4096]{1,0:T(8,128)(2,1)}, f32[128,512]{1,0:T(8,128)}, f32[128,512]{1,0:T(8,128)}, f32[1,4096]{1,0:T(1,128)}, /*index=5*/f32[1,4096]{1,0:T(1,128)}) custom-call(s32[1,128]{1,0:T(1,128)} %bitcast.7, f32[1,4096]{1,0:T(1,128)} %bitcast.5, f32[1,4096]{1,0:T(1,128)} %bitcast.6, ...), custom_call_target="tpu_custom_call" | custom-call | tf_op jit(solution)/shard_map/pallas_call | solution.py:762
  113.1 2.7 %shard_map.119 = (bf16[128,4096]{1,0:T(8,128)(2,1)}, bf16[128,4096]{1,0:T(8,128)(2,1)}, f32[128,512]{1,0:T(8,128)}, f32[128,512]{1,0:T(8,128)}, f32[1,4096]{1,0:T(1,128)}, /*index=5*/f32[1,4096]{1,0:T(1,128)}) custom-call(bf16[128,4096]{1,0:T(8,128)(2,1)} %get-tuple-element.18.refs_0_, bf16[128,4096]{1,0:T(8,128)(2,1)} %get-tuple-element.19.refs_1_, ...), custom_call_target="tpu_custom_call" | custom-call | tf_op jit(solution)/shard_map/pallas_call | solution.py:827

commit v5 on v4

--- a/solution.py
+++ b/solution.py
@@ -588,17 +588,19 @@
 
     both(input_grads_last)
     gains_core()
-    both(weight_grad, 2, 1)
+    weight_grad(0, 2, 1)
     steps(2, 0, 1)
     both(input_grads_mid)
+    weight_grad(1, 2, 1)
     gains_b()
     queries(0)
     steps(2, 2, 3)
     queries(1)
     steps(3, 0, 1)
-    steps(3, 2, 3)
+    steps(3, 2)
+    both(grad_sums)
+    steps(3, 3)
     gains_z()
-    both(grad_sums)
     query_sums(0)
     query_sums(1)
     gains_c()
@@ -617,6 +619,11 @@
         pltpu.make_async_copy(gain_ref.at[0], ggt_out, local.at[4]),
         pltpu.make_async_copy(gain_ref.at[1], ggi_out, local.at[5]),
     ]
+    is_text = jnp.broadcast_to(flag[...], (T, CH)) > 0.5
+    for i in range(S * ZL):
+        at = slice(i * CH, (i + 1) * CH)
+        grads[:, at] = jnp.where(is_text, gt_ref[:, at], gi_ref[:, at])
+
     @pl.loop(0, 2)
     def _(m):
         arrived(df.at[m * 2 + 1 - odd(m)], d2.at[m])
@@ -627,12 +634,12 @@
         normed_grad = dot_nn(place[0], df[half, g]) + dot_nn(place[1], df[2 + half, g])
         for zq in range(ZL):
             at = slice(zq * S * CH + c * CH, zq * S * CH + (c + 1) * CH)
-            gains = jnp.where(flag[...] > 0.5, gt_ref[:, at], gi_ref[:, at])
-            part = normed_grad[:, zq * CH:(zq + 1) * CH] * gains
+            part = normed_grad[:, zq * CH:(zq + 1) * CH] * grads[:, at]
             grads[:, at] = part
             products = products + part * tok_ref[:, at].astype(F32)
     scale = inv[...]
     along = jnp.sum(products, axis=1, keepdims=True) / D * scale * scale
+    scale, along = jnp.broadcast_to(scale, (T, CH)), jnp.broadcast_to(along, (T, CH))
     for i in range(S * ZL):
         at = slice(i * CH, (i + 1) * CH)
         tok_ref[:, at] = (scale * (grads[:, at] - tok_ref[:, at].astype(F32) * along)).astype(BF16)

time: 116 us -> 116 us (level)
  no operation moved by 1% of the time
where the time goes in v5:
time: 116 us
  Pallas kernels  115 us (99%)
    pallas_call x1, Pallas kernels, shards(): pl.pallas_call(functools.partial(layer, dims), out_shape=shapes, in_specs...  112 us
    pallas_call x1, Pallas kernels, shards(): pl.pallas_call(hand_on, out_shape=shapes, in_specs=[anywhere] * 6, out_sp...  2.74 us

profile of v5, /device:TPU:2, one launch (start us, length us, event | category | flops | bytes accessed | tf_op | source)
XLA Modules:
  0.0 116.0 jit_solution(11031687402385709703)
XLA Ops:
  0.6 112.4 %shard_map.118 = (bf16[128,4096]{1,0:T(8,128)(2,1)}, bf16[128,4096]{1,0:T(8,128)(2,1)}, f32[128,512]{1,0:T(8,128)}, f32[128,512]{1,0:T(8,128)}, f32[1,4096]{1,0:T(1,128)}, /*index=5*/f32[1,4096]{1,0:T(1,128)}) custom-call(s32[1,128]{1,0:T(1,128)} %bitcast.7, f32[1,4096]{1,0:T(1,128)} %bitcast.5, f32[1,4096]{1,0:T(1,128)} %bitcast.6, ...), custom_call_target="tpu_custom_call" | custom-call | tf_op jit(solution)/shard_map/pallas_call | solution.py:769
  113.1 2.7 %shard_map.119 = (bf16[128,4096]{1,0:T(8,128)(2,1)}, bf16[128,4096]{1,0:T(8,128)(2,1)}, f32[128,512]{1,0:T(8,128)}, f32[128,512]{1,0:T(8,128)}, f32[1,4096]{1,0:T(1,128)}, /*index=5*/f32[1,4096]{1,0:T(1,128)}) custom-call(bf16[128,4096]{1,0:T(8,128)(2,1)} %get-tuple-element.18.refs_0_, bf16[128,4096]{1,0:T(8,128)(2,1)} %get-tuple-element.19.refs_1_, ...), custom_call_target="tpu_custom_call" | custom-call | tf_op jit(solution)/shard_map/pallas_call | solution.py:834
